TPU v7x, 32 devices: a whole 2x2x4 slice. The times are simulated.
32 devices in a mesh: dp: 4 (over x, core), tensor: 8 (over z, y).
Axes of the slice: x: 2, y: 2, z: 4, core: 2. Of those that a mesh axis runs over, the one named last changes fastest.
Arguments:
- tokens: bfloat16 [2048, 4096], P(('dp', 'tensor')), may hold values from -6 to 6
- cotangent: bfloat16 [2048, 4096], P(('dp', 'tensor')), may hold values from -12 to 12
- loss_mask: int32 [2048], P(('dp', 'tensor')), may hold values from 0 to 1, as said below
- gate_weight: bfloat16 [4096, 14336], P(None, 'tensor'), may hold values from -0.09375 to 0.09375
- up_weight: bfloat16 [4096, 14336], P(None, 'tensor'), may hold values from -0.09375 to 0.09375
- down_weight: bfloat16 [14336, 4096], P('tensor'), may hold values from -0.046875 to 0.046875
- probe_seed: int32 [1], replicated, may hold values from 0 to 1048575
Outputs:
- diag_gate: float32 [4096, 14336], P('dp', 'tensor')
Inputs may be any that keep to these rules, and one draw needn't show every extreme that they name: `loss_mask`: 0 or 1; the first entry is 1.
All inputs are finite; a program needn't handle non-finite values.
Results may differ from a plain program's by a relative error of at most 0.0029.
Values may be sent and summed in bfloat16 or wider, within the bound.
No kernel may reach another device: no remote copies, remote signals or barrier semaphores. Data moves between devices by JAX's collectives and lax.ppermute only.
A program may use at most 192 MiB of HBM per device.

v0:
```python
import jax
import jax.numpy as jnp
from jax import lax
from jax.sharding import PartitionSpec as P

FF = 14336


contract_rows = (((0,), (0,)), ((), ()))
contract_last = (((1,), (1,)), ((), ()))


def probe_signs(seed_value, row_count, col_count, first_col, full_width):
    row_index = lax.broadcasted_iota(jnp.int32, (row_count, col_count), 0)
    col_index = lax.broadcasted_iota(jnp.int32, (row_count, col_count), 1) + first_col
    hashed = (row_index * full_width + col_index) * jnp.int32(-1640531535) + seed_value * jnp.int32(
        668265263
    )
    hashed = hashed ^ lax.shift_right_logical(hashed, jnp.full_like(hashed, 15))
    hashed = hashed * jnp.int32(739982445)
    hashed = hashed ^ lax.shift_right_logical(hashed, jnp.full_like(hashed, 12))
    hashed = hashed * jnp.int32(695872825)
    hashed = hashed ^ lax.shift_right_logical(hashed, jnp.full_like(hashed, 15))
    lowbit = lax.shift_right_logical(hashed, jnp.full_like(hashed, 16)) & jnp.int32(1)
    return jnp.int32(1) - jnp.int32(2) * lowbit


def curvature(gate_pre):
    sigmoid_val = jax.nn.sigmoid(gate_pre)
    return sigmoid_val * (1.0 - sigmoid_val) * (2.0 + gate_pre * (1.0 - 2.0 * sigmoid_val))


def per_device(tokens, cotangent, loss_mask, gate_weight, up_weight, down_weight, probe_seed):
    width_dev = gate_weight.shape[1]
    feature_count = gate_weight.shape[0]
    out_rows = feature_count // lax.axis_size("dp")
    sign_table = probe_signs(
        probe_seed[0], feature_count, width_dev, lax.axis_index("tensor") * width_dev, FF
    )
    probe_bf = sign_table.astype(jnp.bfloat16)
    live_flags = loss_mask.astype(jnp.bfloat16)
    masked = cotangent * live_flags[:, None]
    features = lax.all_gather(tokens, "tensor", axis=0, tiled=True)
    masked_rows = lax.all_gather(masked, "tensor", axis=0, tiled=True)
    live_count = lax.psum(jnp.sum(live_flags.astype(jnp.float32)), ("dp", "tensor"))
    gate_pre = jnp.dot(features, gate_weight, preferred_element_type=jnp.float32)
    up_proj = jnp.dot(features, up_weight, preferred_element_type=jnp.float32)
    tangent = jnp.dot(features, probe_bf, preferred_element_type=jnp.float32)
    back_grad = lax.dot_general(
        masked_rows, down_weight, contract_last, preferred_element_type=jnp.float32
    )
    operand = (back_grad * up_proj * curvature(gate_pre) * tangent).astype(jnp.bfloat16)
    hessian = lax.psum_scatter(
        lax.dot_general(features, operand, contract_rows, preferred_element_type=jnp.float32),
        "dp",
        scatter_dimension=0,
        tiled=True,
    )
    own_signs = lax.dynamic_slice_in_dim(sign_table, lax.axis_index("dp") * out_rows, out_rows, 0)
    return own_signs.astype(jnp.float32) * (hessian / live_count)


def solution(mesh):
    in_specs = (
        P(("dp", "tensor"), None),
        P(("dp", "tensor"), None),
        P(("dp", "tensor")),
        P(None, "tensor"),
        P(None, "tensor"),
        P("tensor", None),
        P(),
    )
    out_specs = P("dp", "tensor")
    return jax.shard_map(
        per_device, mesh=mesh, in_specs=in_specs, out_specs=out_specs, check_vma=False
    )
```

profile of v0, /device:TPU:0, one launch (start us, length us, event | category | flops | bytes accessed | tf_op | source)
XLA Modules:
  0.0 465.5 jit_solution(839322488209407976)
XLA Ops:
  6.5 0.0 all-gather.5.cloned.1.call-start
  6.5 0.7 all-gather.5.cloned.1.call-update
  7.3 0.0 all-gather.3.cloned.1.call-start
  7.3 0.7 convert_element_type.16
  8.0 1.9 broadcast_multiply_fusion
  9.9 0.0 all-gather.3.cloned.1.call-update
  9.9 0.0 reduce-scatter.2.cloned.1.call-start
  10.7 75.0 %all-gather.5.cloned.1.call-done = bf16[512,4096]{1,0:T(8,128)(2,1)} async-done(((bf16[64,4096]{1,0:T(8,128)(2,1)}), bf16[512,4096]{1,0:T(8,128)(2,1)}) %all-gather.5.cloned.1.call-update) | async-done | bytes 4194320 | tf_op jit(solution)/shard_map/all_gather | solution.py:43
  85.6 14.6 %fusion.26 = f32[512,1792]{1,0:T(8,128)} fusion(bf16[512,4096]{1,0:T(8,128)(2,1)} %all-gather.5.cloned.1.call-done, bf16[4096,1792]{1,0:T(8,128)(2,1)} %param.10), kind=kOutput, calls=%fused_computation.35 | convolution fusion | flops 7516192768 | bytes 22544384 | tf_op jit(solution)/shard_map/dot_general | solution.py:46
  100.3 59.2 %all-gather.3.cloned.1.call-done = bf16[512,4096]{1,0:T(8,128)(2,1)} async-done(((bf16[64,4096]{1,0:T(8,128)(2,1)}), bf16[512,4096]{1,0:T(8,128)(2,1)}) %all-gather.3.cloned.1.call-update) | async-done | bytes 4194320 | tf_op jit(solution)/shard_map/all_gather | solution.py:44
  159.4 0.0 copy-start
  159.4 14.7 %fusion.25 = f32[512,1792]{1,0:T(8,128)} fusion(bf16[512,4096]{1,0:T(8,128)(2,1)} %all-gather.3.cloned.1.call-done, bf16[1792,4096]{1,0:T(8,128)(2,1)} %param.12), kind=kOutput, calls=%fused_computation.34 | convolution fusion | flops 7516192768 | bytes 22544384 | tf_op jit(solution)/shard_map/dot_general | solution.py:49
  174.2 0.0 copy-done
  174.2 21.1 %fusion.6 = f32[1792,512]{0,1:T(8,128)} fusion(bf16[512,4096]{1,0:T(8,128)(2,1)S(1)} %copy-done, s32[]{:T(128)} %bitcast, s32[1792]{0:T(1024)S(1)} %iota_add_fusion, s32[4096]{0:T(1024)S(1)} %iota_multiply_fusion), kind=kOutput, calls=%fused_computation.10 | convolution fusion | flops 7633633280 | bytes 7887876 | tf_op jit(solution)/shard_map/dot_general | solution.py:48
  195.3 37.6 %convolution_bitcast_fusion = f32[4096,1792]{0,1:T(8,128)} fusion(bf16[512,4096]{1,0:T(8,128)(2,1)} %all-gather.5.cloned.1.call-done, f32[1792,512]{0,1:T(8,128)} %fusion.6, f32[512,1792]{1,0:T(8,128)} %fusion.26, f32[512,1792]{1,0:T(8,128)} %fusion.25, bf16[4096,1792]{1,0:T(8,128)(2,1)} %param.11), kind=kOutput, calls=%fused_computation.9 | convolution fusion | flops 15045230592 | bytes 59244544 | tf_op jit(solution)/shard_map/dot_general | solution.py:54
  232.9 0.0 copy-start.1
  232.9 0.0 reduce-scatter.2.cloned.1.call-update
  232.9 0.6 copy-done.1
  233.6 0.6 convert_reduce_fusion
  234.2 39.0 %psum.7 = f32[]{:T(128)} all-reduce(f32[]{:T(128)} %convert_reduce_fusion), channel_id=1, replica_groups=mesh['dp'=4,'tensor'=8] {'dp','tensor'}, use_global_device_ids=true, to_apply=%region_2.0 | all-reduce | flops 1 | bytes 8 | tf_op jit(solution)/shard_map/psum | solution.py:45
  273.2 16.8 %fusion.5 = s32[4096,1792]{0,1:T(8,128)} fusion(s32[]{:T(128)} %bitcast, s32[1792]{0:T(1024)S(1)} %iota_add_fusion, s32[4096]{0:T(1024)S(1)} %iota_multiply_fusion), kind=kLoop, calls=%fused_computation.8 | loop fusion | flops 110100480 | bytes 29383684 | tf_op jit(solution)/shard_map/sub | solution.py:25
  290.0 149.2 %reduce-scatter.2.cloned.1.call-done = f32[1024,1792]{0,1:T(8,128)} async-done(((f32[4096,1792]{0,1:T(8,128)}), f32[1024,1792]{0,1:T(8,128)}) %reduce-scatter.2.cloned.1.call-update) | async-done | bytes 7340048 | tf_op jit(solution)/shard_map/reduce_scatter | solution.py:53
  439.2 11.4 %divide_multiply_fusion = f32[1024,1792]{0,1:T(8,128)} fusion(f32[1024,1792]{0,1:T(8,128)} %reduce-scatter.2.cloned.1.call-done, s32[4096,1792]{0,1:T(8,128)} %fusion.5, s32[]{:T(128)S(6)} %select_n.3, f32[]{:T(128)} %psum.7), kind=kLoop, calls=%fused_computation.12 | loop fusion | flops 5505024 | bytes 22020104 | tf_op jit(solution)/shard_map/mul | solution.py:60
  450.7 8.4 %copy.8 = f32[1024,1792]{1,0:T(8,128)} copy(f32[1024,1792]{0,1:T(8,128)} %divide_multiply_fusion) | data formatting | bytes 14680064 | tf_op jit(solution)/shard_map/mul | solution.py:60
  (2 shorter events, 0.0 us)
Async XLA Ops:
  6.5 79.1 %all-gather.5.cloned.1.call-start = ((), (), s32[]{:S(2)}) async-start(), calls=%async_computation.2 | async-start | bytes 4718592 | tf_op jit(solution)/shard_map/all_gather | solution.py:43
  7.3 152.2 %all-gather.3.cloned.1.call-start = ((), (), s32[]{:S(2)}) async-start(), calls=%async_computation.1 | async-start | bytes 4718592 | tf_op jit(solution)/shard_map/all_gather | solution.py:44
  9.9 429.3 %reduce-scatter.2.cloned.1.call-start = ((), (), s32[]{:S(2)}) async-start(), calls=%async_computation.3 | async-start | bytes 36700160 | tf_op jit(solution)/shard_map/reduce_scatter | solution.py:53
  159.4 14.7 %copy-start = (bf16[512,4096]{1,0:T(8,128)(2,1)S(1)}, bf16[512,4096]{1,0:T(8,128)(2,1)}, u32[]{:S(2)}) copy-start(bf16[512,4096]{1,0:T(8,128)(2,1)} %all-gather.5.cloned.1.call-done) | copy-start | bytes 12582916
  232.9 0.7 copy-start.1
Sparse Core Ops, SparseCore 0:
  9.5 76.0 all-gather.4
  87.7 71.6 all-gather.2
  233.1 206.1 reduce-scatter.1
where the time goes:
time: 466 us
  waiting for transfers between devices  284 us (61%)
  matrix products  88.1 us (19%)
  blocking collectives  39 us (8%)
  other arithmetic  31.4 us (7%)
  between operations  13.8 us (3%)
  local copies, waits for them, and re-layouts  9 us (2%)
    reduce_scatter x1, waiting for transfers between devices, per_device(): lax.psum_scatter(lax.dot_general(features, operand, contract_rows, prefer...  149 us
    all_gather x1, waiting for transfers between devices, per_device(): features = lax.all_gather(tokens, 'tensor', axis=0, tiled=True)  75 us
    all_gather x1, waiting for transfers between devices, per_device(): masked_rows = lax.all_gather(masked, 'tensor', axis=0, tiled=True)  59.2 us
    psum x1, blocking collectives, per_device(): lax.psum(jnp.sum(live_flags.astype(jnp.float32)), ('dp', 'tensor'))  39 us
    dot_general x1, matrix products, per_device(): lax.dot_general(features, operand, contract_rows, preferred_element_type=...  37.6 us
    dot_general x1, matrix products, per_device(): tangent = jnp.dot(features, probe_bf, preferred_element_type=jnp.float32)  21.1 us
    sub x1, other arithmetic, probe_signs(): return jnp.int32(1) - jnp.int32(2) * lowbit  16.8 us
    dot_general x1, matrix products, per_device(): lax.dot_general(masked_rows, down_weight, contract_last, preferred_elemen...  14.7 us
  transfers between devices with their start and end apart: 3, of which 3 were waited for; matrix products, arithmetic and copies ran while one was open for 7% of the time, Pallas kernels for 0%

commit v1 on v0

v1 whole, which is shorter than its diff:
```python
import functools

import jax
import jax.numpy as jnp
from jax import lax
from jax.experimental import pallas as pl
from jax.experimental.pallas import tpu as pltpu
from jax.sharding import PartitionSpec as P

FF = 14336
MULT = -1640531535

contract_rows = (((0,), (0,)), ((), ()))
contract_last = (((1,), (1,)), ((), ()))

anywhere = pl.BlockSpec(memory_space=pl.ANY)
in_smem = pl.BlockSpec(memory_space=pltpu.SMEM)
params = pltpu.CompilerParams(vmem_limit_bytes=40 * 1024 * 1024)


def cost(flops, moved):
    return pl.CostEstimate(flops=int(flops), bytes_accessed=int(moved), transcendentals=0)


def mixed_sign(hashed):
    hashed = hashed ^ lax.shift_right_logical(hashed, jnp.full_like(hashed, 15))
    hashed = hashed * jnp.int32(739982445)
    hashed = hashed ^ lax.shift_right_logical(hashed, jnp.full_like(hashed, 12))
    hashed = hashed * jnp.int32(695872825)
    return (hashed ^ lax.shift_left(hashed, jnp.full_like(hashed, 15))) < 0


def column_block(width):
    return 256 if width % 256 == 0 else width


def sign_kernel(start_row, seed_and_col, *rest):
    out = rest[-1]
    rows, width = out.shape
    first = start_row + pl.program_id(0) * rows
    col = lax.broadcasted_iota(jnp.int32, (16, width), 1) + seed_and_col[1]
    row = lax.broadcasted_iota(jnp.int32, (16, width), 0)
    base = (row * FF + col) * jnp.int32(MULT) + seed_and_col[0] * jnp.int32(668265263)

    def chunk(c, carry):
        at = pl.multiple_of(c * 16, 16)
        hashed = base + (first + at) * (jnp.int32(FF) * jnp.int32(MULT))
        out[pl.ds(at, 16), :] = jnp.where(mixed_sign(hashed), -1.0, 1.0).astype(jnp.bfloat16)
        return carry

    lax.fori_loop(0, rows // 16, chunk, 0)


def make_signs(seed_and_col, feature_count, width, part, count, parts, table, deps):
    rows = 256
    steps = feature_count // parts // rows
    given = [] if table is None else [table]
    return pl.pallas_call(
        functools.partial(sign_kernel, part * (feature_count // parts)),
        grid=(steps * count,),
        out_shape=jax.ShapeDtypeStruct((feature_count, width), jnp.bfloat16),
        in_specs=[in_smem] + [anywhere] * (len(given) + len(deps)),
        out_specs=pl.BlockSpec((rows, width), lambda i: (i + part * steps, 0)),
        input_output_aliases={1: 0} if given else {},
        compiler_params=params,
        cost_estimate=cost(feature_count * width * 1200 * count // parts, feature_count * width),
        name="signs",
    )(seed_and_col, *given, *deps)


def curvature(gate_pre):
    sigmoid_val = jax.nn.sigmoid(gate_pre)
    return sigmoid_val * (1.0 - sigmoid_val) * (2.0 + gate_pre * (1.0 - 2.0 * sigmoid_val))


def stack(pieces, scratch):
    @pl.when(pl.program_id(0) == 0)
    def _():
        at = 0
        for piece in pieces:
            scratch[pl.ds(at, piece.shape[0]), :] = piece[...]
            at += piece.shape[0]


def factor_kernel(n_pieces, *refs):
    pieces = refs[:n_pieces]
    gate, up, sign = refs[n_pieces : n_pieces + 3]
    out, scratch = refs[-2:]
    stack(pieces, scratch)
    rows = scratch[...]
    gate_pre = jnp.dot(rows, gate[...], preferred_element_type=jnp.float32)
    up_proj = jnp.dot(rows, up[...], preferred_element_type=jnp.float32)
    tangent = jnp.dot(rows, sign[...], preferred_element_type=jnp.float32)
    out[...] = up_proj * curvature(gate_pre) * tangent


def make_factor(pieces, gate, up, signs, first, count, given, deps):
    depth, width = gate.shape
    block = column_block(width)
    rows = sum(p.shape[0] for p in pieces)
    n = len(pieces)
    given = [] if given is None else [given]
    weight = pl.BlockSpec((depth, block), lambda j: (0, j + first))
    return pl.pallas_call(
        functools.partial(factor_kernel, n),
        grid=(count,),
        out_shape=jax.ShapeDtypeStruct((rows, width), jnp.float32),
        in_specs=[pl.BlockSpec(p.shape, lambda j: (0, 0)) for p in pieces]
        + [weight] * 3
        + [anywhere] * (len(given) + len(deps)),
        out_specs=pl.BlockSpec((rows, block), lambda j: (0, j + first)),
        scratch_shapes=[pltpu.VMEM((rows, depth), jnp.bfloat16)],
        input_output_aliases={n + 3: 0} if given else {},
        compiler_params=params,
        cost_estimate=cost(6 * rows * depth * block * count, 6 * depth * block * count),
        name="factor",
    )(*pieces, gate, up, signs, *given, *deps)


def operand_kernel(n_pieces, n_deps, has_totals, *refs):
    pieces = refs[:n_pieces]
    down, factor = refs[n_pieces : n_pieces + 2]
    outs = refs[n_pieces + 2 + n_deps :]
    out, scratch, turned = outs[0], outs[-2], outs[-1]
    depth = down.shape[1]

    @pl.when(pl.program_id(0) == 0)
    def _():
        at = 0
        for piece in pieces:
            scratch[pl.ds(at, piece.shape[0]), :] = piece[:, :depth]
            at += piece.shape[0]
        turned[...] = scratch[...].T
        if has_totals:
            total = jnp.zeros((16, 128), jnp.float32)
            for piece in pieces:
                total += piece[:16, depth:].astype(jnp.float32)
            outs[1][...] = total

    back_grad = jnp.dot(down[...], turned[...], preferred_element_type=jnp.float32)
    out[...] = (back_grad.T * factor[...]).astype(jnp.bfloat16)


def make_operand(pieces, down, factor, first, count, has_totals, deps):
    width, depth = down.shape
    block = column_block(width)
    rows = factor.shape[0]
    n = len(pieces)
    out_shape = [jax.ShapeDtypeStruct((rows, block * count), jnp.bfloat16)]
    out_specs = [pl.BlockSpec((rows, block), lambda j: (0, j))]
    if has_totals:
        out_shape.append(jax.ShapeDtypeStruct((16, 128), jnp.float32))
        out_specs.append(pl.BlockSpec((16, 128), lambda j: (0, 0)))
    made = pl.pallas_call(
        functools.partial(operand_kernel, n, len(deps), has_totals),
        grid=(count,),
        out_shape=out_shape,
        in_specs=[pl.BlockSpec(p.shape, lambda j: (0, 0)) for p in pieces]
        + [
            pl.BlockSpec((block, depth), lambda j: (j + first, 0)),
            pl.BlockSpec((rows, block), lambda j: (0, j + first)),
        ]
        + [anywhere] * len(deps),
        out_specs=out_specs,
        scratch_shapes=[
            pltpu.VMEM((rows, depth), jnp.bfloat16),
            pltpu.VMEM((depth, rows), jnp.bfloat16),
        ],
        compiler_params=params,
        cost_estimate=cost(2 * rows * depth * block * count, 2 * depth * block * count),
        name="operand",
    )(*pieces, down, factor, *deps)
    return made if has_totals else (made[0], None)


def turn_kernel(*refs):
    out, scratch = refs[-2:]
    at = 0
    for part in refs[:-2]:
        scratch[pl.ds(at, part.shape[0]), :] = part[...]
        at += part.shape[0]
    out[...] = scratch[...].T


def turn_parts(parts):
    whole = pl.BlockSpec(memory_space=pltpu.VMEM)
    rows = sum(p.shape[0] for p in parts)
    cols = parts[0].shape[1]
    return pl.pallas_call(
        turn_kernel,
        out_shape=jax.ShapeDtypeStruct((cols, rows), jnp.bfloat16),
        in_specs=[whole] * len(parts),
        out_specs=whole,
        scratch_shapes=[pltpu.VMEM((rows, cols), jnp.bfloat16)],
        compiler_params=params,
        cost_estimate=cost(3e9, 4 * rows * cols),
        name="turn",
    )(*parts)


def hessian_kernel(n, finish, dp_ref, *refs):
    turned, operands = refs[0], refs[1 : n + 1]
    out, gathered = refs[-2:]
    at = 0
    for operand in operands:
        gathered[pl.ds(at, operand.shape[0]), :] = operand[...]
        at += operand.shape[0]
    total = jnp.dot(turned[...], gathered[...], preferred_element_type=jnp.float32)
    if finish:
        base, sign, totals = refs[n + 1 : n + 4]
        scale = 1.0 / totals[0:1, 0:1]
        total = (total + base[...]) * scale * sign[...].astype(jnp.float32)
    out[...] = total


def make_hessian(turned, operands, dp, first, width, finish, given, deps):
    out_rows, rows = turned.shape
    block = column_block(width)
    count = operands[0].shape[1] // block
    n = len(operands)
    given = [] if given is None else [given]
    extra_specs = [
        pl.BlockSpec((out_rows, block), lambda j, dp_ref: (0, j + first)),
        pl.BlockSpec((out_rows, block), lambda j, dp_ref: (dp_ref[0], j + first)),
        pl.BlockSpec((16, 128), lambda j, dp_ref: (0, 0)),
    ]
    return pl.pallas_call(
        functools.partial(hessian_kernel, n, bool(finish)),
        grid_spec=pltpu.PrefetchScalarGridSpec(
            num_scalar_prefetch=1,
            grid=(count,),
            in_specs=[pl.BlockSpec(turned.shape, lambda j, dp_ref: (0, 0))]
            + [pl.BlockSpec((o.shape[0], block), lambda j, dp_ref: (0, j)) for o in operands]
            + extra_specs[: len(finish)]
            + [anywhere] * (len(given) + len(deps)),
            out_specs=pl.BlockSpec((out_rows, block), lambda j, dp_ref: (0, j + first)),
            scratch_shapes=[pltpu.VMEM((rows, block), jnp.bfloat16)],
        ),
        out_shape=jax.ShapeDtypeStruct((out_rows, width), jnp.float32),
        input_output_aliases={n + 2 + len(finish): 0} if given else {},
        compiler_params=params,
        cost_estimate=cost(2 * rows * out_rows * block * count, 8 * out_rows * block * count),
        name="hessian",
    )(dp, turned, *operands, *finish, *given, *deps)


def nothing(*refs):
    pass


def after(value, deps):
    return pl.pallas_call(
        nothing,
        out_shape=jax.ShapeDtypeStruct(value.shape, value.dtype),
        in_specs=[anywhere] * (1 + len(deps)),
        out_specs=anywhere,
        input_output_aliases={0: 0},
        cost_estimate=cost(1e6, 1e3),
        name="after",
    )(value, *deps)


def take_kernel(n, at_ref, *refs):
    out, at = refs[-1], 0
    for piece in refs[:n]:
        out[pl.ds(at, piece.shape[0]), :] = piece[...]
        at += piece.shape[0]


def take_columns(pieces, at, width, deps):
    rows = sum(p.shape[0] for p in pieces)
    return pl.pallas_call(
        functools.partial(take_kernel, len(pieces)),
        grid_spec=pltpu.PrefetchScalarGridSpec(
            num_scalar_prefetch=1,
            grid=(1,),
            in_specs=[
                pl.BlockSpec((p.shape[0], width), lambda j, at_ref: (0, at_ref[0])) for p in pieces
            ]
            + [anywhere] * len(deps),
            out_specs=pl.BlockSpec((rows, width), lambda j, at_ref: (0, 0)),
        ),
        out_shape=jax.ShapeDtypeStruct((rows, width), pieces[0].dtype),
        compiler_params=params,
        cost_estimate=cost(2e9, 4 * rows * width),
        name="columns",
    )(at.astype(jnp.int32).reshape(1), *pieces, *deps)


def mask_kernel(rows, flags, *rest):
    rest[-1][...] = rows[...] * flags[...]


def masked_rows(rows, flags, deps):
    whole = pl.BlockSpec(memory_space=pltpu.VMEM)
    return pl.pallas_call(
        mask_kernel,
        out_shape=jax.ShapeDtypeStruct(rows.shape, rows.dtype),
        in_specs=[whole, whole] + [anywhere] * len(deps),
        out_specs=whole,
        compiler_params=params,
        name="masked",
    )(rows, jnp.broadcast_to(flags[:, None], rows.shape[:1] + (128,))[:, :1], *deps)


def ranks(mask, rows):
    before = lax.broadcasted_iota(jnp.int32, (rows, rows), 0) < lax.broadcasted_iota(
        jnp.int32, (rows, rows), 1
    )
    return jnp.dot(mask, before.astype(jnp.float32), preferred_element_type=jnp.float32)


def pack_kernel(rows, mask, kept, excess):
    size = rows.shape[0]
    live = mask[...].astype(jnp.float32)
    rank = ranks(live, size).astype(jnp.int32)
    slot = lax.broadcasted_iota(jnp.int32, (size, size), 0)
    pick = jnp.where((slot == rank) & (live > 0.5), 1.0, 0.0).astype(jnp.bfloat16)
    packed = jnp.dot(pick, rows[...], preferred_element_type=jnp.float32).astype(jnp.bfloat16)
    cap = kept.shape[0]
    kept[...] = packed[:cap]
    excess[...] = packed[cap:]


def pack_live(rows, mask, cap):
    whole = pl.BlockSpec(memory_space=pltpu.VMEM)
    return pl.pallas_call(
        pack_kernel,
        out_shape=[
            jax.ShapeDtypeStruct((cap, rows.shape[1]), rows.dtype),
            jax.ShapeDtypeStruct((rows.shape[0] - cap, rows.shape[1]), rows.dtype),
        ],
        in_specs=[whole, whole],
        out_specs=[whole, whole],
        compiler_params=params,
        cost_estimate=cost(2e9, 2 * rows.size * 2),
        name="pack",
    )(rows, mask)


def place_kernel(stat_in, *refs):
    kept, received, mask = refs[:3]
    out, left = refs[-2 - (not stat_in) :][:2]
    cap, more = kept.shape[0], received.shape[0]
    depth = kept.shape[1]
    live = jnp.sum(mask[...].astype(jnp.float32), axis=1, keepdims=True)
    first = jnp.minimum(live.astype(jnp.int32), cap)

    def moved(rows, start):
        slot = lax.broadcasted_iota(jnp.int32, (rows, more), 0) + start
        source = lax.broadcasted_iota(jnp.int32, (rows, more), 1) + first
        pick = jnp.where(slot == source, 1.0, 0.0).astype(jnp.bfloat16)
        return jnp.dot(pick, received[...], preferred_element_type=jnp.float32)

    rest = moved(more, cap)
    left[...] = rest.astype(jnp.bfloat16)
    out[:, :depth] = kept[...] + moved(cap, 0).astype(jnp.bfloat16)
    if stat_in:
        stat = refs[3]
        row = lax.broadcasted_iota(jnp.int32, (cap, 128), 0)
        lanes = jnp.where(row == 0, stat[0:1, :], jnp.where(row == 1, stat[1:2, :], 0.0))
        out[:, depth:] = lanes.astype(jnp.bfloat16)
    else:
        row = lax.broadcasted_iota(jnp.int32, (8, 128), 0)
        any_left = jnp.max(jnp.max(jnp.abs(rest), axis=1, keepdims=True), axis=0, keepdims=True)
        flag = jnp.where(any_left > 0.0, 1.0, 0.0)
        refs[-1][...] = jnp.where(row == 0, live, jnp.where(row == 1, flag, 0.0))


def place_rows(kept, received, mask, stat, deps):
    whole = pl.BlockSpec(memory_space=pltpu.VMEM)
    cap, depth = kept.shape
    given = [] if stat is None else [stat]
    out_shape = [
        jax.ShapeDtypeStruct((cap, depth + 128 * len(given)), kept.dtype),
        jax.ShapeDtypeStruct(received.shape, kept.dtype),
    ]
    if stat is None:
        out_shape.append(jax.ShapeDtypeStruct((8, 128), jnp.float32))
    return pl.pallas_call(
        functools.partial(place_kernel, stat is not None),
        out_shape=out_shape,
        in_specs=[whole] * (3 + len(given)) + [anywhere] * len(deps),
        out_specs=[whole] * len(out_shape),
        compiler_params=params,
        cost_estimate=cost(2e9, 2 * kept.size * 2),
        name="place",
    )(kept, received, mask, *given, *deps)


def sum_steps(value, axis):
    size = lax.axis_size(axis)
    if size & (size - 1):
        return [lax.psum(value, axis)]
    step, values = 1, []
    while step < size:
        value = value + lax.ppermute(value, axis, [(i, (i + step) % size) for i in range(size)])
        values.append(value)
        step *= 2
    return values


def gather_steps(piece, late):
    size = lax.axis_size("tensor")
    if size != 8:
        rows = lax.all_gather(piece, "tensor", axis=0, tiled=True)
        half = rows.shape[0] // 2
        return [rows[:half]], [rows[half:]], [[], [], []]
    step = [(i, (i + 2) % size) for i in range(size)]
    swap = [(i, i ^ 1) for i in range(size)]
    later = after(piece, late) if late else piece
    z = [piece]
    for k in range(3):
        z.append(lax.ppermute(z[-1] if k else later, "tensor", step))
    y = [lax.ppermute(p, "tensor", swap) for p in z[:3]]
    if late:
        y.append(lax.ppermute(later, "tensor", [(i, (i + 6) % size ^ 1) for i in range(size)]))
    else:
        y.append(lax.ppermute(z[3], "tensor", swap))
    marks = [[z[1], y[0]], [z[2], y[1]], [z[3], y[2]]]
    if late:
        marks[2] = [y[3]]
    return [z[0], y[0], z[1], y[1]], [z[2], y[2], z[3], y[3]], marks


def per_device(tokens, cotangent, loss_mask, gate_weight, up_weight, down_weight, probe_seed):
    depth, width = gate_weight.shape
    n_dp = lax.axis_size("dp")
    n_x = n_dp // 2
    out_rows = depth // n_dp
    dp = lax.axis_index("dp")
    first_col = lax.axis_index("tensor") * width
    seed_and_col = jnp.stack([probe_seed[0], first_col.astype(jnp.int32)])
    blocks = width // column_block(width)
    ends = [0, (blocks + 1) // 2, blocks]
    cuts = [(lo, hi - lo) for lo, hi in zip(ends, ends[1:]) if hi > lo]
    rows_dev = tokens.shape[0]
    cap = -(-3 * rows_dev // 64) * 16
    packing = cap < rows_dev and n_dp * rows_dev <= 256

    def move(i, j):
        return [(s, ((s // 2 + i) % n_x) * 2 + ((s % 2) ^ j)) for s in range(n_dp)]

    def spread_tokens(pieces, deps, later):
        def columns(piece, at, size):
            return lax.dynamic_slice_in_dim(piece, at, size, 1)

        chip, core = dp // 2, dp % 2
        received = []
        for i in range(1, n_x):
            sent = take_columns(pieces, (chip + i) % n_x, 2 * out_rows, deps)
            received.append(lax.ppermute(sent, "dp", move(i, 0)))

        if later:
            received = [after(r, later) for r in received]

        def of_core(c):
            return jnp.concatenate(
                [columns(p, (chip * 2 + c) * out_rows, out_rows) for p in pieces]
                + [columns(r, c * out_rows, out_rows) for r in received],
                axis=0,
            )

        return [of_core(core), lax.ppermute(of_core(1 - core), "dp", move(0, 1))]

    def spread_operand(operand, deps=()):
        parts = [lax.ppermute(operand, "dp", move(i, 0)) for i in range(1, n_x)]
        if deps:
            parts = [after(p, deps) for p in parts]
        parts = [operand] + parts
        return parts + [lax.ppermute(p, "dp", move(0, 1)) for p in parts]

    if packing:
        mirror = [(s, n_dp - 1 - s) for s in range(n_dp)]
        mask_row = loss_mask.reshape(1, rows_dev)
        kept, excess = pack_live(tokens, mask_row, cap)
        received = lax.ppermute(excess, "dp", mirror)
        kept_cot, excess_cot = pack_live(cotangent, mask_row, cap)
        received_cot = lax.ppermute(excess_cot, "dp", mirror)
        tokens, left, stat = place_rows(kept, received, mask_row, None, [])
    else:
        stat = jnp.zeros((8, 128), jnp.float32) + jnp.sum(loss_mask.astype(jnp.float32))
    stats = sum_steps(stat, "dp")
    early = [received_cot] if packing else []

    tok_a, tok_b, tok_marks = gather_steps(tokens, [])
    signs = None
    for first, count, deps in (
        (0, 1, [kept_cot] if packing else []),
        (1, 2, [tokens]),
        (3, 2, stats[:1] + early),
        (5, 3, tok_marks[0] + stats[-1:]),
    ):
        signs = make_signs(seed_and_col, depth, width, first, count, 8, signs, deps)
    if packing:
        masked, left_cot = place_rows(
            kept_cot, received_cot, mask_row, stats[-1], tok_marks[0]
        )
    else:
        masked = masked_rows(cotangent, loss_mask.astype(jnp.bfloat16), tok_marks[2])
    cot_a, cot_b, cot_marks = gather_steps(masked, tok_marks[2])

    def factor_of(tok, at, given, deps):
        if at >= len(cuts):
            return given
        first, count = cuts[at]
        return make_factor(tok, gate_weight, up_weight, signs, first, count, given, deps)

    factor_a = factor_of(tok_a, 0, None, tok_marks[1])
    factor_a = factor_of(tok_a, 1, factor_a, tok_marks[2] + cot_marks[0][1:])
    parts_a = spread_tokens(tok_a, [], [factor_a])
    factor_b = factor_of(tok_b, 0, None, cot_marks[0] + [factor_a])
    operand_a, totals = make_operand(
        cot_a, down_weight, factor_a, 0, blocks, packing, cot_marks[1] + parts_a + [factor_b]
    )
    parts_b = spread_tokens(tok_b, [factor_a], [operand_a])
    factor_b = factor_of(tok_b, 1, factor_b, [operand_a] + cot_marks[2])
    operands_a = spread_operand(operand_a, [factor_b])
    chunks, before = [], [operand_a, operands_a[n_x], parts_b[1]]
    for first, count in cuts:
        made, more = make_operand(
            cot_b, down_weight, factor_b, first, count, packing and first == 0, before
        )
        before = [made] + operands_a[1:]
        if more is not None:
            totals = totals + more
        chunks.append((first, made))
    if not packing:
        totals = jnp.zeros((16, 128), jnp.float32) + sum_steps(stats[-1], "tensor")[-1][0, 0]
    turned_a, turned_b = turn_parts(parts_a), turn_parts(parts_b)
    dp_at = dp.astype(jnp.int32).reshape(1)
    base = make_hessian(turned_a, operands_a, dp_at, 0, width, (), None, before)
    spread = [
        spread_operand(made, [] if k else [base]) for k, (first, made) in enumerate(chunks)
    ]
    out = None
    for (first, made), operands in zip(chunks, spread):
        others = [p[1] for p in spread if p is not operands] if out is None else []
        out = make_hessian(
            turned_b, operands, dp_at, first, width, (base, signs, totals), out, others
        )
    if not packing:
        return out

    def second_round(done):
        features = jnp.concatenate(sum(gather_steps(left, [])[:2], []), axis=0)
        rest = jnp.concatenate(sum(gather_steps(left_cot, [])[:2], []), axis=0)
        gate_pre = jnp.dot(features, gate_weight, preferred_element_type=jnp.float32)
        up_proj = jnp.dot(features, up_weight, preferred_element_type=jnp.float32)
        tangent = jnp.dot(features, signs, preferred_element_type=jnp.float32)
        back_grad = lax.dot_general(
            rest, down_weight, contract_last, preferred_element_type=jnp.float32
        )
        operand = (back_grad * up_proj * curvature(gate_pre) * tangent).astype(jnp.bfloat16)
        more = lax.dot_general(
            jnp.concatenate(spread_tokens([features], [], []), axis=0),
            jnp.concatenate(spread_operand(operand), axis=0),
            contract_rows,
            preferred_element_type=jnp.float32,
        )
        own_signs = lax.dynamic_slice_in_dim(signs, dp * out_rows, out_rows, 0)
        return done + more / totals[0, 0] * own_signs.astype(jnp.float32)

    return lax.cond(totals[1, 0] > 0.5, second_round, lambda done: done, out)


def solution(mesh):
    in_specs = (
        P(("dp", "tensor"), None),
        P(("dp", "tensor"), None),
        P(("dp", "tensor")),
        P(None, "tensor"),
        P(None, "tensor"),
        P("tensor", None),
        P(),
    )
    out_specs = P("dp", "tensor")
    return jax.shard_map(
        per_device, mesh=mesh, in_specs=in_specs, out_specs=out_specs, check_vma=False
    )
```

time: 466 us -> 177 us (0.38)
  waiting for transfers between devices: 284 us -> 11.2 us
  Pallas kernels: 0 us -> 104 us
  matrix products: 88.1 us -> 0 us
  blocking collectives: 39 us -> 0 us
  other arithmetic: 31.4 us -> 0.09 us
  starting transfers between devices: 0.08 us -> 29.3 us
  local copies, waits for them, and re-layouts: 9 us -> 29.4 us
  between operations: 13.8 us -> 1.95 us
    reduce_scatter x1 -> x0, waiting for transfers between devices: 149 us -> none  [per_device(): lax.psum_scatter(lax.dot_general(features, operand, contract_rows, prefer...]
    all_gather x2 -> x0, waiting for transfers between devices: 134 us -> none  [the longest x1 75 us: per_device(): features = lax.all_gather(tokens, 'tensor', axis=0, tiled=True)]
    pallas_call x0 -> x27, Pallas kernels: none -> 104 us  [the longest x4 39.4 us: make_factor(): pl.pallas_call(functools.partial(factor_kernel, n), grid=(count,), out_sh...]
    dot_general x4 -> x0, matrix products: 88.1 us -> none  [the longest x1 37.6 us: per_device(): lax.dot_general(features, operand, contract_rows, preferred_element_type=...]
    psum x1 -> x0, blocking collectives: 39 us -> none  [per_device(): lax.psum(jnp.sum(live_flags.astype(jnp.float32)), ('dp', 'tensor'))]
    ppermute x0 -> x31, starting transfers between devices: none -> 29.3 us  [the longest x6 7.14 us: gather_steps(): y = [lax.ppermute(p, 'tensor', swap) for p in z[:3]]]
    unnamed x4 -> x83, local copies, waits for them, and re-layouts: 0.63 us -> 24.8 us
    sub x1 -> x0, other arithmetic: 16.8 us -> none  [probe_signs(): return jnp.int32(1) - jnp.int32(2) * lowbit]
  transfers between devices with their start and end apart: 3 -> 31, of which waited for: 3 -> 4; matrix products, arithmetic and copies ran while one was open for 7% -> 6% of each run, Pallas kernels for 0% -> 55%
where the time goes in v1:
time: 177 us; the launch traced here: 176 us
  Pallas kernels  104 us (59%)
  local copies, waits for them, and re-layouts  29.4 us (17%)
  starting transfers between devices  29.3 us (17%)
  waiting for transfers between devices  11.2 us (6%)
  between operations  1.95 us (1%)
    pallas_call x4, Pallas kernels, make_factor(): pl.pallas_call(functools.partial(factor_kernel, n), grid=(count,), out_sh...  39.4 us
    pallas_call x3, Pallas kernels, make_operand(): pl.pallas_call(functools.partial(operand_kernel, n, len(deps), has_totals...  24.8 us
    unnamed x83, local copies, waits for them, and re-layouts  24.8 us
    pallas_call x3, Pallas kernels, make_hessian(): pl.pallas_call(functools.partial(hessian_kernel, n, bool(finish)), grid_s...  16.6 us
    pallas_call x4, Pallas kernels, make_signs(): pl.pallas_call(functools.partial(sign_kernel, part * (feature_count // pa...  15.7 us
    ppermute x6, starting transfers between devices, gather_steps(): y = [lax.ppermute(p, 'tensor', swap) for p in z[:3]]  7.14 us
    ppermute x6, starting transfers between devices, gather_steps(): z.append(lax.ppermute(z[-1] if k else later, 'tensor', step))  7.1 us
    ppermute x6, waiting for transfers between devices, gather_steps(): y = [lax.ppermute(p, 'tensor', swap) for p in z[:3]]  6.89 us
  transfers between devices with their start and end apart: 31, of which 4 were waited for; matrix products, arithmetic and copies ran while one was open for 6% of the time, Pallas kernels for 55%

profile of v1, /device:TPU:0, one launch (start us, length us, event | category | flops | bytes accessed | tf_op | source)
XLA Modules:
  0.0 175.8 jit_solution(2678180976375471457)
XLA Ops:
  2.1 2.4 %collective-permute-start.20 = (bf16[16,4096]{1,0:T(8,128)(2,1)S(1)}, bf16[16,4096]{1,0:T(8,128)(2,1)S(1)}, u32[]{:S(2)}, u32[]{:S(2)}) collective-permute-start(bf16[16,4096]{1,0:T(8,128)(2,1)S(1)} %get-tuple-element.52), channel_id=1, source_target_pairs={{0,24},{8,16},{16,8},{24,0},{1,25},{9,17},{17,9},{25,1},{2,26},{10... | collective-permute-start | bytes 393224 | tf_op jit(solution)/shard_map/ppermute | solution.py:477
  6.3 2.2 %signs.4.rest_0_ = bf16[4096,1792]{1,0:T(8,128)(2,1)S(1)} custom-call(s32[2]{0:T(128)S(1)} %pad_add_fusion.seed_and_col, bf16[48,4096]{1,0:T(8,128)(2,1)S(1)} %get-tuple-element.49.refs_0_.rest_0_), custom_call_target="tpu_custom_call" | custom-call | flops 1101004800 | bytes 7340032 | tf_op jit(solution)/shard_map/signs/pallas_call | solution.py:58
  9.5 2.4 %collective-permute-start.23 = (bf16[48,4096]{1,0:T(8,128)(2,1)S(1)}, bf16[48,4096]{1,0:T(8,128)(2,1)S(1)}, u32[]{:S(2)}, u32[]{:S(2)}) collective-permute-start(bf16[48,4096]{1,0:T(8,128)(2,1)S(1)} %get-tuple-element.54.rest_1_.refs_0_), channel_id=1, source_target_pairs={{0,2},{1,3},{2,4},{3,5},{4,6},{5,7},{6,0},{7,1},{8,10},{9,11},{10,... | collective-permute-start | bytes 1179656 | tf_op jit(solution)/shard_map/ppermute | solution.py:414
  13.4 3.9 %signs.5.rest_0_ = bf16[4096,1792]{1,0:T(8,128)(2,1)S(1)} custom-call(s32[2]{0:T(128)S(1)} %pad_add_fusion.seed_and_col, bf16[4096,1792]{1,0:T(8,128)(2,1)S(1)} %signs.4.rest_0_, bf16[48,4096]{1,0:T(8,128)(2,1)S(1)} %get-tuple-element.54.rest_1_.refs_0_), custom_call_target="tpu_custom_call", output_to_operand_aliasing={{}: (1, {})} | custom-call | flops 2202009600 | bytes 7340032 | tf_op jit(solution)/shard_map/signs/pallas_call | solution.py:58
  17.4 3.0 %collective-permute-done.21 = f32[8,128]{1,0:T(8,128)S(1)} collective-permute-done((f32[8,128]{1,0:T(8,128)S(1)}, f32[8,128]{1,0:T(8,128)S(1)}, u32[]{:S(2)}, u32[]{:S(2)}) %collective-permute-start.21) | collective-permute-done | bytes 4128 | tf_op jit(solution)/shard_map/ppermute | solution.py:397
  21.9 3.9 %signs.6.rest_0_ = bf16[4096,1792]{1,0:T(8,128)(2,1)S(1)} custom-call(s32[2]{0:T(128)S(1)} %pad_add_fusion.seed_and_col, bf16[4096,1792]{1,0:T(8,128)(2,1)S(1)} %signs.5.rest_0_, f32[8,128]{1,0:T(8,128)S(1)} %add.111.rest_1_, bf16[16,4096]{1,0:T(8,128)(2,1)S(1)} %collective-permute-done.19.refs_1_.rest_2_), custom_call_target="tpu_custom_call", output_to_operand_aliasing={{}: (1, {})} | custom-call | flops 2202009600 | bytes 7340032 | tf_op jit(solution)/shard_map/signs/pallas_call | solution.py:58
  27.5 1.8 %copy.35.refs_0_ = bf16[48,4224]{1,0:T(8,128)(2,1)} copy(bf16[48,4224]{1,0:T(8,128)(2,1)} %get-tuple-element.55.refs_0_) | data formatting | bytes 811008
  32.5 5.6 %signs.7.refs_6_ = bf16[4096,1792]{1,0:T(8,128)(2,1)S(1)} custom-call(s32[2]{0:T(128)S(1)} %pad_add_fusion.seed_and_col, bf16[4096,1792]{1,0:T(8,128)(2,1)S(1)} %signs.6.rest_0_, bf16[48,4096]{1,0:T(8,128)(2,1)S(1)} %collective-permute-done.23.refs_4_.rest_1_.refs_2_, ...), custom_call_target="tpu_custom_call", output_to_operand_aliasing={{}: (1, {})} | custom-call | flops 3303014400 | bytes 7340032 | tf_op jit(solution)/shard_map/signs/pallas_call | solution.py:58
  38.1 6.9 %collective-permute-done.31.refs_3_.refs_8_ = bf16[48,4096]{1,0:T(8,128)(2,1)S(1)} collective-permute-done((bf16[48,4096]{1,0:T(8,128)(2,1)S(1)}, bf16[48,4096]{1,0:T(8,128)(2,1)S(1)}, u32[]{:S(2)}, u32[]{:S(2)}) %collective-permute-start.31) | collective-permute-done | bytes 393248 | tf_op jit(solution)/shard_map/ppermute | solution.py:415
  50.4 9.7 %factor.4.refs_7_ = f32[192,1792]{1,0:T(8,128)S(1)} custom-call(bf16[48,4096]{1,0:T(8,128)(2,1)S(1)} %get-tuple-element.54.rest_1_.refs_0_, bf16[48,4096]{1,0:T(8,128)(2,1)S(1)} %collective-permute-done.24.refs_5_.rest_2_.refs_1_, bf16[48,4096]{1,0:T(8,128)(2,1)S(1)} %collective-permute-done.23.refs_4_.rest_1_.refs_2_, ...), custom_call_target="tpu_custom_call" | custom-call | flops 4831838208 | bytes 25165824 | tf_op jit(solution)/shard_map/factor/pallas_call | solution.py:104
  63.3 3.2 %collective-permute-start.38 = (bf16[48,4224]{1,0:T(8,128)(2,1)}, bf16[48,4224]{1,0:T(8,128)(2,1)}, u32[]{:S(2)}, u32[]{:S(2)}) collective-permute-start(bf16[48,4224]{1,0:T(8,128)(2,1)} %after.5), channel_id=1, source_target_pairs={{0,7},{1,6},{2,1},{3,0},{4,3},{5,2},{6,5},{7,4},{8,15},{9,14},{10,... | collective-permute-start | bytes 1216520 | tf_op jit(solution)/shard_map/ppermute | solution.py:417
  71.0 8.9 %factor.5.refs_1_.refs_9_.refs_5_.refs_4_ = f32[192,1792]{1,0:T(8,128)S(1)} custom-call(bf16[48,4096]{1,0:T(8,128)(2,1)S(1)} %get-tuple-element.54.rest_1_.refs_0_, bf16[48,4096]{1,0:T(8,128)(2,1)S(1)} %copy-done.18, bf16[48,4096]{1,0:T(8,128)(2,1)S(1)} %collective-permute-done.23.refs_4_.rest_1_.refs_2_, ...), custom_call_target="tpu_custom_call", output_to_operand_aliasing={{}: (7, {})} | custom-call | flops 3623878656 | bytes 18874368 | tf_op jit(solution)/shard_map/factor/pallas_call | solution.py:104
  80.9 2.1 %dynamic-slice_dynamic-update-slice_fusion.2 = (bf16[384,1024]{1,0:T(8,128)(2,1)}, bf16[384,1024]{1,0:T(8,128)(2,1)}) fusion(bf16[384,1024]{1,0:T(8,128)(2,1)} %copy-done.35, bf16[192,2048]{1,0:T(8,128)(2,1)} %after.6, s32[]{:T(128)S(6)} %select_n.80, bf16[384,1024]{1,0:T(8,128)(2,1)} %copy-done.24, s32[]{:T(128)S(6)} %select_n.78), kind=kLoop, calls=%fused_computation.43 | loop fusion | bytes 1572872 | tf_op jit(solution)/shard_map/concatenate | solution.py:458
  88.9 11.5 %factor.6.refs_10_.refs_7_ = f32[192,1792]{1,0:T(8,128)S(1)} custom-call(bf16[48,4096]{1,0:T(8,128)(2,1)S(1)} %collective-permute-done.26.refs_7_.refs_0_, bf16[48,4096]{1,0:T(8,128)(2,1)S(1)} %copy-done.14, bf16[48,4096]{1,0:T(8,128)(2,1)S(1)} %copy-done.11, bf16[48,4096]{1,0:T(8,128)(2,1)} %collective-permute-done.35.refs_3_, bf16[4096,1792]{1,0:T(8,128)(2,1)} %refs_4_.11, ...), custom_call_target="tpu_custom_call" | custom-call | flops 4831838208 | bytes 25165824 | tf_op jit(solution)/shard_map/factor/pallas_call | solution.py:104
  100.9 11.8 %operand.3 = (bf16[192,1792]{1,0:T(8,128)(2,1)}, f32[16,128]{1,0:T(8,128)S(1)}) custom-call(bf16[48,4224]{1,0:T(8,128)(2,1)} %get-tuple-element.55.refs_0_, bf16[48,4224]{1,0:T(8,128)(2,1)} %collective-permute-done.25.refs_10_.refs_8_.refs_1_, bf16[48,4224]{1,0:T(8,128)(2,1)} %collective-permute-done.29.refs_7_.refs_2_, ...), custom_call_target="tpu_custom_call" | custom-call | flops 2818572288 | bytes 14680064 | tf_op jit(solution)/shard_map/operand/pallas_call | solution.py:154
  115.9 2.1 %dynamic-slice_dynamic-update-slice_fusion = (bf16[384,1024]{1,0:T(8,128)(2,1)}, bf16[384,1024]{1,0:T(8,128)(2,1)}) fusion(bf16[384,1024]{1,0:T(8,128)(2,1)} %get-tuple-element.73, bf16[192,2048]{1,0:T(8,128)(2,1)} %after.7, s32[]{:T(128)S(6)} %select_n.78, bf16[384,1024]{1,0:T(8,128)(2,1)} %get-tuple-element.74, s32[]{:T(128)S(6)} %select_n.80), kind=kLoop, calls=%fused_computation.41 | loop fusion | bytes 1572872 | tf_op jit(solution)/shard_map/concatenate | solution.py:458
  121.0 9.4 %factor.7.refs_5_.refs_1_ = f32[192,1792]{1,0:T(8,128)S(1)} custom-call(bf16[48,4096]{1,0:T(8,128)(2,1)S(1)} %copy-done.16, bf16[48,4096]{1,0:T(8,128)(2,1)S(1)} %copy-done.14, bf16[48,4096]{1,0:T(8,128)(2,1)S(1)} %copy-done.11, bf16[48,4096]{1,0:T(8,128)(2,1)} %collective-permute-done.35.refs_3_, ...), custom_call_target="tpu_custom_call", output_to_operand_aliasing={{}: (7, {})} | custom-call | flops 3623878656 | bytes 18874368 | tf_op jit(solution)/shard_map/factor/pallas_call | solution.py:104
  135.5 7.3 %operand.4 = (bf16[192,1024]{1,0:T(8,128)(2,1)}, f32[16,128]{1,0:T(8,128)S(1)}) custom-call(bf16[48,4224]{1,0:T(8,128)(2,1)S(1)} %copy-done.22, bf16[48,4224]{1,0:T(8,128)(2,1)} %collective-permute-done.36.refs_1_, bf16[48,4224]{1,0:T(8,128)(2,1)} %collective-permute-done.37.refs_2_, bf16[48,4224]{1,0:T(8,128)(2,1)} %collective-permute-done.38.refs_9_.refs_3_, ...), custom_call_target="tpu_custom_call" | custom-call | flops 1610612736 | bytes 8388608 | tf_op jit(solution)/shard_map/operand/pallas_call | solution.py:154
  144.4 5.7 %operand.5.refs_5_.refs_1_ = bf16[192,768]{1,0:T(8,128)(2,1)S(1)} custom-call(bf16[48,4224]{1,0:T(8,128)(2,1)S(1)} %copy-done.23, bf16[48,4224]{1,0:T(8,128)(2,1)} %collective-permute-done.36.refs_1_, bf16[48,4224]{1,0:T(8,128)(2,1)} %collective-permute-done.37.refs_2_, bf16[48,4224]{1,0:T(8,128)(2,1)} %collective-permute-done.38.refs_9_.refs_3_, ...), custom_call_target="tpu_custom_call" | custom-call | flops 1207959552 | bytes 6291456 | tf_op jit(solution)/shard_map/operand/pallas_call | solution.py:154
  151.3 6.1 %hessian.3.refs_1_.refs_5_ = f32[1024,1792]{1,0:T(8,128)S(1)} custom-call(s32[1]{0:T(128)} %bitcast.6.dp_ref, bf16[1024,768]{1,0:T(8,128)(2,1)S(1)} %turn.3.refs_0_, bf16[192,1792]{1,0:T(8,128)(2,1)} %get-tuple-element.57.refs_8_.refs_1_.refs_6_, bf16[192,1792]{1,0:T(8,128)(2,1)S(1)} %copy-done.8, ...), custom_call_target="tpu_custom_call" | custom-call | flops 2818572288 | bytes 14680064 | tf_op jit(solution)/shard_map/hessian/pallas_call | solution.py:227
  157.5 3.0 %copy-done = f32[1024,1792]{1,0:T(8,128)} copy-done((f32[1024,1792]{1,0:T(8,128)}, f32[1024,1792]{1,0:T(8,128)S(1)}, u32[]{:S(2)}) %copy-start) | copy-done | bytes 7340056
  162.6 2.0 %turn.2.refs_0_ = bf16[1024,768]{1,0:T(8,128)(2,1)S(1)} custom-call(bf16[384,1024]{1,0:T(8,128)(2,1)} %get-tuple-element.69.refs_0_, bf16[384,1024]{1,0:T(8,128)(2,1)} %collective-permute-done.41.refs_8_.refs_1_), custom_call_target="tpu_custom_call" | custom-call | flops 3000000000 | bytes 3145728 | tf_op jit(solution)/shard_map/turn/pallas_call | solution.py:189
  165.2 5.7 %hessian.4.refs_8_ = f32[1024,1792]{1,0:T(8,128)} custom-call(s32[1]{0:T(128)} %bitcast.6.dp_ref, bf16[1024,768]{1,0:T(8,128)(2,1)S(1)} %turn.2.refs_0_, bf16[192,1024]{1,0:T(8,128)(2,1)} %get-tuple-element.59.refs_6_.refs_1_, bf16[192,1024]{1,0:T(8,128)(2,1)} %after.9.refs_2_, bf16[192,1024]{1,0:T(8,128)(2,1)} %collective-permute-done.48.refs_3_, ...), custom_call_target="tpu_custom_call" | custom-call | flops 1610612736 | bytes 8388608 | tf_op jit(solution)/shard_map/hessian/pallas_call | solution.py:227
  170.9 4.8 %hessian.5 = f32[1024,1792]{1,0:T(8,128)} custom-call(s32[1]{0:T(128)} %bitcast.6.dp_ref, bf16[1024,768]{1,0:T(8,128)(2,1)S(1)} %turn.2.refs_0_, bf16[192,768]{1,0:T(8,128)(2,1)S(1)} %operand.5.refs_5_.refs_1_, bf16[192,768]{1,0:T(8,128)(2,1)} %collective-permute-done.44.refs_8_.refs_2_, ...), custom_call_target="tpu_custom_call", output_to_operand_aliasing={{}: (9, {})} | custom-call | flops 1207959552 | bytes 6291456 | tf_op jit(solution)/shard_map/hessian/pallas_call | solution.py:227
  (157 shorter events, 48.4 us)
Async XLA Ops:
  5.0 16.9 %collective-permute-start.19 = (bf16[16,4096]{1,0:T(8,128)(2,1)S(1)}, bf16[16,4096]{1,0:T(8,128)(2,1)S(1)}, u32[]{:S(2)}, u32[]{:S(2)}) collective-permute-start(bf16[16,4096]{1,0:T(8,128)(2,1)S(1)} %get-tuple-element.50), channel_id=1, source_target_pairs={{0,24},{8,16},{16,8},{24,0},{1,25},{9,17},{17,9},{25,1},{2,26},{10... | collective-permute-start | bytes 393224 | tf_op jit(solution)/shard_map/ppermute | solution.py:479
  9.5 16.4 %collective-permute-start.23 = (bf16[48,4096]{1,0:T(8,128)(2,1)S(1)}, bf16[48,4096]{1,0:T(8,128)(2,1)S(1)}, u32[]{:S(2)}, u32[]{:S(2)}) collective-permute-start(bf16[48,4096]{1,0:T(8,128)(2,1)S(1)} %get-tuple-element.54.rest_1_.refs_0_), channel_id=1, source_target_pairs={{0,2},{1,3},{2,4},{3,5},{4,6},{5,7},{6,0},{7,1},{8,10},{9,11},{10,... | collective-permute-start | bytes 1179656 | tf_op jit(solution)/shard_map/ppermute | solution.py:414
  11.9 14.0 %collective-permute-start.24 = (bf16[48,4096]{1,0:T(8,128)(2,1)S(1)}, bf16[48,4096]{1,0:T(8,128)(2,1)S(1)}, u32[]{:S(2)}, u32[]{:S(2)}) collective-permute-start(bf16[48,4096]{1,0:T(8,128)(2,1)S(1)} %get-tuple-element.54.rest_1_.refs_0_), channel_id=1, source_target_pairs={{0,1},{1,0},{2,3},{3,2},{4,5},{5,4},{6,7},{7,6},{8,9},{9,8},{10,11... | collective-permute-start | bytes 1179656 | tf_op jit(solution)/shard_map/ppermute | solution.py:415
  27.0 40.0 %collective-permute-start.25 = (bf16[48,4224]{1,0:T(8,128)(2,1)}, bf16[48,4224]{1,0:T(8,128)(2,1)}, u32[]{:S(2)}, u32[]{:S(2)}) collective-permute-start(bf16[48,4224]{1,0:T(8,128)(2,1)} %get-tuple-element.55.refs_0_), channel_id=1, source_target_pairs={{0,1},{1,0},{2,3},{3,2},{4,5},{5,4},{6,7},{7,6},{8,9},{9,8},{10,11... | collective-permute-start | bytes 1216520 | tf_op jit(solution)/shard_map/ppermute | solution.py:415
  29.4 18.2 %collective-permute-start.26 = (bf16[48,4096]{1,0:T(8,128)(2,1)S(1)}, bf16[48,4096]{1,0:T(8,128)(2,1)S(1)}, u32[]{:S(2)}, u32[]{:S(2)}) collective-permute-start(bf16[48,4096]{1,0:T(8,128)(2,1)S(1)} %collective-permute-done.23.refs_4_.rest_1_.refs_2_), channel_id=1, source_target_pairs={{0,2},{1,3},{2,4},{3,5},{4,6},{5,7},{6,0},{7,1},{8,10},{9,11},{10,... | collective-permute-start | bytes 1179656 | tf_op jit(solution)/shard_map/ppermute | solution.py:414
  30.9 14.1 %collective-permute-start.31 = (bf16[48,4096]{1,0:T(8,128)(2,1)S(1)}, bf16[48,4096]{1,0:T(8,128)(2,1)S(1)}, u32[]{:S(2)}, u32[]{:S(2)}) collective-permute-start(bf16[48,4096]{1,0:T(8,128)(2,1)S(1)} %collective-permute-done.23.refs_4_.rest_1_.refs_2_), channel_id=1, source_target_pairs={{0,1},{1,0},{2,3},{3,2},{4,5},{5,4},{6,7},{7,6},{8,9},{9,8},{10,11... | collective-permute-start | bytes 1179656 | tf_op jit(solution)/shard_map/ppermute | solution.py:415
  46.1 34.9 %collective-permute-start.33 = (bf16[192,2048]{1,0:T(8,128)(2,1)}, bf16[192,2048]{1,0:T(8,128)(2,1)}, u32[]{:S(2)}, u32[]{:S(2)}) collective-permute-start(bf16[192,2048]{1,0:T(8,128)(2,1)} %columns.4), channel_id=1, source_target_pairs={{0,16},{8,24},{16,0},{24,8},{1,17},{9,25},{17,1},{25,9},{2,18},{10... | collective-permute-start | bytes 2359304 | tf_op jit(solution)/shard_map/ppermute | solution.py:452
  47.5 12.6 %collective-permute-start.27 = (bf16[48,4096]{1,0:T(8,128)(2,1)S(1)}, bf16[48,4096]{1,0:T(8,128)(2,1)S(1)}, u32[]{:S(2)}, u32[]{:S(2)}) collective-permute-start(bf16[48,4096]{1,0:T(8,128)(2,1)S(1)} %collective-permute-done.26.refs_7_.refs_0_), channel_id=1, source_target_pairs={{0,2},{1,3},{2,4},{3,5},{4,6},{5,7},{6,0},{7,1},{8,10},{9,11},{10,... | collective-permute-start | bytes 1179656 | tf_op jit(solution)/shard_map/ppermute | solution.py:414
  61.7 25.7 %collective-permute-start.29 = (bf16[48,4224]{1,0:T(8,128)(2,1)}, bf16[48,4224]{1,0:T(8,128)(2,1)}, u32[]{:S(2)}, u32[]{:S(2)}) collective-permute-start(bf16[48,4224]{1,0:T(8,128)(2,1)} %after.5), channel_id=1, source_target_pairs={{0,2},{1,3},{2,4},{3,5},{4,6},{5,7},{6,0},{7,1},{8,10},{9,11},{10,... | collective-permute-start | bytes 1216520 | tf_op jit(solution)/shard_map/ppermute | solution.py:414
  63.3 56.8 %collective-permute-start.38 = (bf16[48,4224]{1,0:T(8,128)(2,1)}, bf16[48,4224]{1,0:T(8,128)(2,1)}, u32[]{:S(2)}, u32[]{:S(2)}) collective-permute-start(bf16[48,4224]{1,0:T(8,128)(2,1)} %after.5), channel_id=1, source_target_pairs={{0,7},{1,6},{2,1},{3,0},{4,3},{5,2},{6,5},{7,4},{8,15},{9,14},{10,... | collective-permute-start | bytes 1216520 | tf_op jit(solution)/shard_map/ppermute | solution.py:417
  66.5 18.0 %collective-permute-start.35 = (bf16[48,4096]{1,0:T(8,128)(2,1)}, bf16[48,4096]{1,0:T(8,128)(2,1)}, u32[]{:S(2)}, u32[]{:S(2)}) collective-permute-start(bf16[48,4096]{1,0:T(8,128)(2,1)} %copy-done.9), channel_id=1, source_target_pairs={{0,1},{1,0},{2,3},{3,2},{4,5},{5,4},{6,7},{7,6},{8,9},{9,8},{10,11... | collective-permute-start | bytes 1179656 | tf_op jit(solution)/shard_map/ppermute | solution.py:419
  83.0 17.9 %collective-permute-start.34 = (bf16[384,1024]{1,0:T(8,128)(2,1)}, bf16[384,1024]{1,0:T(8,128)(2,1)S(1)}, u32[]{:S(2)}, u32[]{:S(2)}) collective-permute-start(bf16[384,1024]{1,0:T(8,128)(2,1)} %get-tuple-element.71), channel_id=1, source_target_pairs={{0,8},{8,0},{16,24},{24,16},{1,9},{9,1},{17,25},{25,17},{2,10},{10... | collective-permute-start | bytes 2359304 | tf_op jit(solution)/shard_map/ppermute | solution.py:464
  86.8 29.1 %collective-permute-start.40 = (bf16[192,2048]{1,0:T(8,128)(2,1)S(1)}, bf16[192,2048]{1,0:T(8,128)(2,1)}, u32[]{:S(2)}, u32[]{:S(2)}) collective-permute-start(bf16[192,2048]{1,0:T(8,128)(2,1)S(1)} %columns.5), channel_id=1, source_target_pairs={{0,16},{8,24},{16,0},{24,8},{1,17},{9,25},{17,1},{25,9},{2,18},{10... | collective-permute-start | bytes 2359304 | tf_op jit(solution)/shard_map/ppermute | solution.py:452
  87.4 13.5 %collective-permute-start.32 = (bf16[48,4224]{1,0:T(8,128)(2,1)}, bf16[48,4224]{1,0:T(8,128)(2,1)S(1)}, u32[]{:S(2)}, u32[]{:S(2)}) collective-permute-start(bf16[48,4224]{1,0:T(8,128)(2,1)} %collective-permute-done.29.refs_7_.refs_2_), channel_id=1, source_target_pairs={{0,2},{1,3},{2,4},{3,5},{4,6},{5,7},{6,0},{7,1},{8,10},{9,11},{10,... | collective-permute-start | bytes 1216520 | tf_op jit(solution)/shard_map/ppermute | solution.py:414
  87.4 13.5 %collective-permute-start.30 = (bf16[48,4224]{1,0:T(8,128)(2,1)}, bf16[48,4224]{1,0:T(8,128)(2,1)S(1)}, u32[]{:S(2)}, u32[]{:S(2)}) collective-permute-start(bf16[48,4224]{1,0:T(8,128)(2,1)} %collective-permute-done.29.refs_7_.refs_2_), channel_id=1, source_target_pairs={{0,1},{1,0},{2,3},{3,2},{4,5},{5,4},{6,7},{7,6},{8,9},{9,8},{10,11... | collective-permute-start | bytes 1216520 | tf_op jit(solution)/shard_map/ppermute | solution.py:415
  112.7 18.8 %collective-permute-start.42 = (bf16[192,1792]{1,0:T(8,128)(2,1)}, bf16[192,1792]{1,0:T(8,128)(2,1)S(1)}, u32[]{:S(2)}, u32[]{:S(2)}) collective-permute-start(bf16[192,1792]{1,0:T(8,128)(2,1)} %get-tuple-element.57.refs_8_.refs_1_.refs_6_), channel_id=1, source_target_pairs={{0,16},{8,24},{16,0},{24,8},{1,17},{9,25},{17,1},{25,9},{2,18},{10... | collective-permute-start | bytes 2064392 | tf_op jit(solution)/shard_map/ppermute | solution.py:467
  118.0 15.2 %collective-permute-start.41 = (bf16[384,1024]{1,0:T(8,128)(2,1)}, bf16[384,1024]{1,0:T(8,128)(2,1)}, u32[]{:S(2)}, u32[]{:S(2)}) collective-permute-start(bf16[384,1024]{1,0:T(8,128)(2,1)} %get-tuple-element.70), channel_id=1, source_target_pairs={{0,8},{8,0},{16,24},{24,16},{1,9},{9,1},{17,25},{25,17},{2,10},{10... | collective-permute-start | bytes 2359304 | tf_op jit(solution)/shard_map/ppermute | solution.py:464
  118.0 15.2 %collective-permute-start.39 = (bf16[192,1792]{1,0:T(8,128)(2,1)}, bf16[192,1792]{1,0:T(8,128)(2,1)S(1)}, u32[]{:S(2)}, u32[]{:S(2)}) collective-permute-start(bf16[192,1792]{1,0:T(8,128)(2,1)} %get-tuple-element.57.refs_8_.refs_1_.refs_6_), channel_id=1, source_target_pairs={{0,8},{8,0},{16,24},{24,16},{1,9},{9,1},{17,25},{25,17},{2,10},{10... | collective-permute-start | bytes 2064392 | tf_op jit(solution)/shard_map/ppermute | solution.py:471
  118.5 13.9 %collective-permute-start.36 = (bf16[48,4224]{1,0:T(8,128)(2,1)}, bf16[48,4224]{1,0:T(8,128)(2,1)}, u32[]{:S(2)}, u32[]{:S(2)}) collective-permute-start(bf16[48,4224]{1,0:T(8,128)(2,1)} %copy-done.21), channel_id=1, source_target_pairs={{0,1},{1,0},{2,3},{3,2},{4,5},{5,4},{6,7},{7,6},{8,9},{9,8},{10,11... | collective-permute-start | bytes 1216520 | tf_op jit(solution)/shard_map/ppermute | solution.py:415
  120.0 13.1 %collective-permute-start.37 = (bf16[48,4224]{1,0:T(8,128)(2,1)}, bf16[48,4224]{1,0:T(8,128)(2,1)}, u32[]{:S(2)}, u32[]{:S(2)}) collective-permute-start(bf16[48,4224]{1,0:T(8,128)(2,1)} %copy-done.21), channel_id=1, source_target_pairs={{0,2},{1,3},{2,4},{3,5},{4,6},{5,7},{6,0},{7,1},{8,10},{9,11},{10,... | collective-permute-start | bytes 1216520 | tf_op jit(solution)/shard_map/ppermute | solution.py:414
  132.3 11.6 %collective-permute-start.43 = (bf16[192,1792]{1,0:T(8,128)(2,1)}, bf16[192,1792]{1,0:T(8,128)(2,1)S(1)}, u32[]{:S(2)}, u32[]{:S(2)}) collective-permute-start(bf16[192,1792]{1,0:T(8,128)(2,1)} %after.8.refs_7_.refs_2_.refs_6_), channel_id=1, source_target_pairs={{0,8},{8,0},{16,24},{24,16},{1,9},{9,1},{17,25},{25,17},{2,10},{10... | collective-permute-start | bytes 2064392 | tf_op jit(solution)/shard_map/ppermute | solution.py:471
  142.8 17.7 %collective-permute-start.47 = (bf16[192,1024]{1,0:T(8,128)(2,1)}, bf16[192,1024]{1,0:T(8,128)(2,1)}, u32[]{:S(2)}, u32[]{:S(2)}) collective-permute-start(bf16[192,1024]{1,0:T(8,128)(2,1)} %get-tuple-element.59.refs_6_.refs_1_), channel_id=1, source_target_pairs={{0,16},{8,24},{16,0},{24,8},{1,17},{9,25},{17,1},{25,9},{2,18},{10... | collective-permute-start | bytes 1179656 | tf_op jit(solution)/shard_map/ppermute | solution.py:467
  143.9 20.7 %collective-permute-start.48 = (bf16[192,1024]{1,0:T(8,128)(2,1)}, bf16[192,1024]{1,0:T(8,128)(2,1)}, u32[]{:S(2)}, u32[]{:S(2)}) collective-permute-start(bf16[192,1024]{1,0:T(8,128)(2,1)} %get-tuple-element.59.refs_6_.refs_1_), channel_id=1, source_target_pairs={{0,8},{8,0},{16,24},{24,16},{1,9},{9,1},{17,25},{25,17},{2,10},{10... | collective-permute-start | bytes 1179656 | tf_op jit(solution)/shard_map/ppermute | solution.py:471
  150.1 12.1 %collective-permute-start.44 = (bf16[192,768]{1,0:T(8,128)(2,1)S(1)}, bf16[192,768]{1,0:T(8,128)(2,1)}, u32[]{:S(2)}, u32[]{:S(2)}) collective-permute-start(bf16[192,768]{1,0:T(8,128)(2,1)S(1)} %operand.5.refs_5_.refs_1_), channel_id=1, source_target_pairs={{0,16},{8,24},{16,0},{24,8},{1,17},{9,25},{17,1},{25,9},{2,18},{10... | collective-permute-start | bytes 884744 | tf_op jit(solution)/shard_map/ppermute | solution.py:467
  (44 other events, 303.1 us)

commit v2 on v1

--- a/solution.py
+++ b/solution.py
@@ -51,19 +51,19 @@
     lax.fori_loop(0, rows // 16, chunk, 0)
 
 
-def make_signs(seed_and_col, feature_count, width, part, count, parts, table, deps):
+def make_signs(seed_and_col, feature_count, width, part, parts, table, deps):
     rows = 256
     steps = feature_count // parts // rows
     given = [] if table is None else [table]
     return pl.pallas_call(
         functools.partial(sign_kernel, part * (feature_count // parts)),
-        grid=(steps * count,),
+        grid=(steps,),
         out_shape=jax.ShapeDtypeStruct((feature_count, width), jnp.bfloat16),
         in_specs=[in_smem] + [anywhere] * (len(given) + len(deps)),
         out_specs=pl.BlockSpec((rows, width), lambda i: (i + part * steps, 0)),
         input_output_aliases={1: 0} if given else {},
         compiler_params=params,
-        cost_estimate=cost(feature_count * width * 1200 * count // parts, feature_count * width),
+        cost_estimate=cost(feature_count * width * 1200 // parts, feature_count * width),
         name="signs",
     )(seed_and_col, *given, *deps)
 
@@ -400,7 +400,7 @@
     return values
 
 
-def gather_steps(piece, late):
+def gather_steps(piece, straight):
     size = lax.axis_size("tensor")
     if size != 8:
         rows = lax.all_gather(piece, "tensor", axis=0, tiled=True)
@@ -408,17 +408,16 @@
         return [rows[:half]], [rows[half:]], [[], [], []]
     step = [(i, (i + 2) % size) for i in range(size)]
     swap = [(i, i ^ 1) for i in range(size)]
-    later = after(piece, late) if late else piece
     z = [piece]
     for k in range(3):
-        z.append(lax.ppermute(z[-1] if k else later, "tensor", step))
+        z.append(lax.ppermute(z[-1], "tensor", step))
     y = [lax.ppermute(p, "tensor", swap) for p in z[:3]]
-    if late:
-        y.append(lax.ppermute(later, "tensor", [(i, (i + 6) % size ^ 1) for i in range(size)]))
+    if straight:
+        y.append(lax.ppermute(piece, "tensor", [(i, (i + 6) % size ^ 1) for i in range(size)]))
     else:
         y.append(lax.ppermute(z[3], "tensor", swap))
     marks = [[z[1], y[0]], [z[2], y[1]], [z[3], y[2]]]
-    if late:
+    if straight:
         marks[2] = [y[3]]
     return [z[0], y[0], z[1], y[1]], [z[2], y[2], z[3], y[3]], marks
 
@@ -441,7 +440,7 @@
     def move(i, j):
         return [(s, ((s // 2 + i) % n_x) * 2 + ((s % 2) ^ j)) for s in range(n_dp)]
 
-    def spread_tokens(pieces, deps, later):
+    def spread_tokens(pieces, deps):
         def columns(piece, at, size):
             return lax.dynamic_slice_in_dim(piece, at, size, 1)
 
@@ -450,9 +449,6 @@
         for i in range(1, n_x):
             sent = take_columns(pieces, (chip + i) % n_x, 2 * out_rows, deps)
             received.append(lax.ppermute(sent, "dp", move(i, 0)))
-
-        if later:
-            received = [after(r, later) for r in received]
 
         def of_core(c):
             return jnp.concatenate(
@@ -483,22 +479,19 @@
     stats = sum_steps(stat, "dp")
     early = [received_cot] if packing else []
 
-    tok_a, tok_b, tok_marks = gather_steps(tokens, [])
-    signs = None
-    for first, count, deps in (
-        (0, 1, [kept_cot] if packing else []),
-        (1, 2, [tokens]),
-        (3, 2, stats[:1] + early),
-        (5, 3, tok_marks[0] + stats[-1:]),
-    ):
-        signs = make_signs(seed_and_col, depth, width, first, count, 8, signs, deps)
+    tok_a, tok_b, tok_marks = gather_steps(tokens, False)
+    signs = make_signs(seed_and_col, depth, width, 0, 4, None, [tokens])
+    signs = make_signs(seed_and_col, depth, width, 1, 4, signs, stats[:1] + early)
+    signs = make_signs(seed_and_col, depth, width, 2, 4, signs, tok_marks[0] + stats[-1:])
+    signs = make_signs(seed_and_col, depth, width, 3, 4, signs, [])
     if packing:
         masked, left_cot = place_rows(
-            kept_cot, received_cot, mask_row, stats[-1], tok_marks[0]
+            kept_cot, received_cot, mask_row, stats[-1], tok_marks[2] + [signs]
         )
     else:
-        masked = masked_rows(cotangent, loss_mask.astype(jnp.bfloat16), tok_marks[2])
-    cot_a, cot_b, cot_marks = gather_steps(masked, tok_marks[2])
+        masked = masked_rows(cotangent, loss_mask.astype(jnp.bfloat16), tok_marks[2] + [signs])
+    cot_a, cot_b, cot_marks = gather_steps(masked, True)
+    parts_a = spread_tokens(tok_a, [])
 
     def factor_of(tok, at, given, deps):
         if at >= len(cuts):
@@ -507,21 +500,20 @@
         return make_factor(tok, gate_weight, up_weight, signs, first, count, given, deps)
 
     factor_a = factor_of(tok_a, 0, None, tok_marks[1])
-    factor_a = factor_of(tok_a, 1, factor_a, tok_marks[2] + cot_marks[0][1:])
-    parts_a = spread_tokens(tok_a, [], [factor_a])
-    factor_b = factor_of(tok_b, 0, None, cot_marks[0] + [factor_a])
+    factor_a = factor_of(tok_a, 1, factor_a, tok_marks[2] + [masked])
+    factor_b = factor_of(tok_b, 0, None, cot_marks[0][:1] + [factor_a])
+    parts_b = spread_tokens(tok_b, [factor_b])
     operand_a, totals = make_operand(
         cot_a, down_weight, factor_a, 0, blocks, packing, cot_marks[1] + parts_a + [factor_b]
     )
-    parts_b = spread_tokens(tok_b, [factor_a], [operand_a])
-    factor_b = factor_of(tok_b, 1, factor_b, [operand_a] + cot_marks[2])
+    factor_b = factor_of(tok_b, 1, factor_b, [operand_a] + cot_b[1:3])
     operands_a = spread_operand(operand_a, [factor_b])
-    chunks, before = [], [operand_a, operands_a[n_x], parts_b[1]]
+    chunks, before = [], [operand_a]
     for first, count in cuts:
         made, more = make_operand(
             cot_b, down_weight, factor_b, first, count, packing and first == 0, before
         )
-        before = [made] + operands_a[1:]
+        before = [made]
         if more is not None:
             totals = totals + more
         chunks.append((first, made))
@@ -543,8 +535,8 @@
         return out
 
     def second_round(done):
-        features = jnp.concatenate(sum(gather_steps(left, [])[:2], []), axis=0)
-        rest = jnp.concatenate(sum(gather_steps(left_cot, [])[:2], []), axis=0)
+        features = jnp.concatenate(sum(gather_steps(left, False)[:2], []), axis=0)
+        rest = jnp.concatenate(sum(gather_steps(left_cot, False)[:2], []), axis=0)
         gate_pre = jnp.dot(features, gate_weight, preferred_element_type=jnp.float32)
         up_proj = jnp.dot(features, up_weight, preferred_element_type=jnp.float32)
         tangent = jnp.dot(features, signs, preferred_element_type=jnp.float32)
@@ -553,7 +545,7 @@
         )
         operand = (back_grad * up_proj * curvature(gate_pre) * tangent).astype(jnp.bfloat16)
         more = lax.dot_general(
-            jnp.concatenate(spread_tokens([features], [], []), axis=0),
+            jnp.concatenate(spread_tokens([features], []), axis=0),
             jnp.concatenate(spread_operand(operand), axis=0),
             contract_rows,
             preferred_element_type=jnp.float32,

time: 177 us -> 165 us (0.932)
  local copies, waits for them, and re-layouts: 29.4 us -> 13.7 us
  Pallas kernels: 104 us -> 106 us
    unnamed x83 -> x50, local copies, waits for them, and re-layouts: 24.8 us -> 11.1 us
    ppermute x6, waiting for transfers between devices: 6.89 us -> 0.55 us  [gather_steps(): y = [lax.ppermute(p, 'tensor', swap) for p in z[:3]]]
    ppermute x1, waiting for transfers between devices: 0.01 us -> 4.98 us  [gather_steps(): y.append(lax.ppermute(z[3], 'tensor', swap))]
    pallas_call x4, Pallas kernels: 15.7 us -> 20 us  [make_signs(): pl.pallas_call(functools.partial(sign_kernel, part * (feature_count // pa...]
    ppermute x3, waiting for transfers between devices: 0.01 us -> 3.14 us  [spread_operand(): parts = [lax.ppermute(operand, 'dp', move(i, 0)) for i in range(1, n_x)]]
    ppermute x2, waiting for transfers between devices: 2.99 us -> 0.01 us  [sum_steps(): lax.ppermute(value, axis, [(i, (i + step) % size) for i in range(size)])]
    ppermute x1, waiting for transfers between devices: 0.01 us -> 2.1 us  [per_device(): received = lax.ppermute(excess, 'dp', mirror)]
    concatenate x2, local copies, waits for them, and re-layouts: 4.14 us -> 2.1 us  [of_core(): jnp.concatenate([columns(p, (chip * 2 + c) * out_rows, out_rows) for p in...]
  transfers between devices with their start and end apart: 31 -> 31, of which waited for: 4 -> 5; matrix products, arithmetic and copies ran while one was open for 6% -> 2% of each run, Pallas kernels for 55% -> 61%
where the time goes in v2:
time: 165 us; the launch traced here: 164 us
  Pallas kernels  106 us (64%)
  starting transfers between devices  29.8 us (18%)
  local copies, waits for them, and re-layouts  13.7 us (8%)
  waiting for transfers between devices  12.7 us (8%)
  between operations  1.84 us (1%)
    pallas_call x4, Pallas kernels, make_factor(): pl.pallas_call(functools.partial(factor_kernel, n), grid=(count,), out_sh...  39.8 us
    pallas_call x3, Pallas kernels, make_operand(): pl.pallas_call(functools.partial(operand_kernel, n, len(deps), has_totals...  23.8 us
    pallas_call x4, Pallas kernels, make_signs(): pl.pallas_call(functools.partial(sign_kernel, part * (feature_count // pa...  20 us
    pallas_call x3, Pallas kernels, make_hessian(): pl.pallas_call(functools.partial(hessian_kernel, n, bool(finish)), grid_s...  16.9 us
    unnamed x50, local copies, waits for them, and re-layouts  11.1 us
    ppermute x6, starting transfers between devices, gather_steps(): z.append(lax.ppermute(z[-1], 'tensor', step))  8.66 us
    ppermute x6, starting transfers between devices, gather_steps(): y = [lax.ppermute(p, 'tensor', swap) for p in z[:3]]  6.27 us
    ppermute x1, waiting for transfers between devices, gather_steps(): y.append(lax.ppermute(z[3], 'tensor', swap))  4.98 us
  transfers between devices with their start and end apart: 31, of which 5 were waited for; matrix products, arithmetic and copies ran while one was open for 2% of the time, Pallas kernels for 61%

profile of v2, /device:TPU:0, one launch (start us, length us, event | category | flops | bytes accessed | tf_op | source)
XLA Modules:
  0.0 164.5 jit_solution(2835205436328651424)
XLA Ops:
  2.1 2.4 %collective-permute-start.20 = (bf16[16,4096]{1,0:T(8,128)(2,1)S(1)}, bf16[16,4096]{1,0:T(8,128)(2,1)S(1)}, u32[]{:S(2)}, u32[]{:S(2)}) collective-permute-start(bf16[16,4096]{1,0:T(8,128)(2,1)S(1)} %get-tuple-element.52), channel_id=1, source_target_pairs={{0,24},{8,16},{16,8},{24,0},{1,25},{9,17},{17,9},{25,1},{2,26},{10... | collective-permute-start | bytes 393224 | tf_op jit(solution)/shard_map/ppermute | solution.py:473
  6.3 2.1 %collective-permute-done.20.refs_1_ = bf16[16,4096]{1,0:T(8,128)(2,1)S(1)} collective-permute-done((bf16[16,4096]{1,0:T(8,128)(2,1)S(1)}, bf16[16,4096]{1,0:T(8,128)(2,1)S(1)}, u32[]{:S(2)}, u32[]{:S(2)}) %collective-permute-start.20) | collective-permute-done | bytes 131104 | tf_op jit(solution)/shard_map/ppermute | solution.py:473
  9.3 2.5 %collective-permute-start.23 = (bf16[48,4096]{1,0:T(8,128)(2,1)S(1)}, bf16[48,4096]{1,0:T(8,128)(2,1)S(1)}, u32[]{:S(2)}, u32[]{:S(2)}) collective-permute-start(bf16[48,4096]{1,0:T(8,128)(2,1)S(1)} %get-tuple-element.54.rest_0_.refs_0_), channel_id=1, source_target_pairs={{0,2},{1,3},{2,4},{3,5},{4,6},{5,7},{6,0},{7,1},{8,10},{9,11},{10,... | collective-permute-start | bytes 1179656 | tf_op jit(solution)/shard_map/ppermute | solution.py:413
  13.4 4.9 %signs.4.rest_0_ = bf16[4096,1792]{1,0:T(8,128)(2,1)} custom-call(s32[2]{0:T(128)S(1)} %pad_add_fusion.seed_and_col, bf16[48,4096]{1,0:T(8,128)(2,1)S(1)} %get-tuple-element.54.rest_0_.refs_0_), custom_call_target="tpu_custom_call" | custom-call | flops 2202009600 | bytes 7340032 | tf_op jit(solution)/shard_map/signs/pallas_call | solution.py:58
  20.0 5.0 %signs.5.rest_0_ = bf16[4096,1792]{1,0:T(8,128)(2,1)} custom-call(s32[2]{0:T(128)S(1)} %pad_add_fusion.seed_and_col, bf16[4096,1792]{1,0:T(8,128)(2,1)} %signs.4.rest_0_, f32[8,128]{1,0:T(8,128)S(1)} %add.111.rest_1_, bf16[16,4096]{1,0:T(8,128)(2,1)S(1)} %collective-permute-done.19.rest_2_.refs_1_), custom_call_target="tpu_custom_call", output_to_operand_aliasing={{}: (1, {})} | custom-call | flops 2202009600 | bytes 7340032 | tf_op jit(solution)/shard_map/signs/pallas_call | solution.py:58
  27.2 5.0 %signs.6.rest_0_ = bf16[4096,1792]{1,0:T(8,128)(2,1)} custom-call(s32[2]{0:T(128)S(1)} %pad_add_fusion.seed_and_col, bf16[4096,1792]{1,0:T(8,128)(2,1)} %signs.5.rest_0_, bf16[48,4096]{1,0:T(8,128)(2,1)S(1)} %collective-permute-done.23.rest_1_.refs_2_, bf16[48,4096]{1,0:T(8,128)(2,1)S(1)} %collective-permute-done.27.rest_2_.refs_1_, ...), custom_call_target="tpu_custom_call", output_to_operand_aliasing={{}: (1, {})} | custom-call | flops 2202009600 | bytes 7340032 | tf_op jit(solution)/shard_map/signs/pallas_call | solution.py:58
  32.2 5.0 %signs.7.refs_6_ = bf16[4096,1792]{1,0:T(8,128)(2,1)} custom-call(s32[2]{0:T(128)S(1)} %pad_add_fusion.seed_and_col, bf16[4096,1792]{1,0:T(8,128)(2,1)} %signs.6.rest_0_), custom_call_target="tpu_custom_call", output_to_operand_aliasing={{}: (1, {})} | custom-call | flops 2202009600 | bytes 7340032 | tf_op jit(solution)/shard_map/signs/pallas_call | solution.py:58
  41.3 10.8 %factor.4.refs_7_ = f32[192,1792]{1,0:T(8,128)S(1)} custom-call(bf16[48,4096]{1,0:T(8,128)(2,1)S(1)} %get-tuple-element.54.rest_0_.refs_0_, bf16[48,4096]{1,0:T(8,128)(2,1)S(1)} %collective-permute-done.27.rest_2_.refs_1_, bf16[48,4096]{1,0:T(8,128)(2,1)S(1)} %collective-permute-done.23.rest_1_.refs_2_, ...), custom_call_target="tpu_custom_call" | custom-call | flops 4831838208 | bytes 25165824 | tf_op jit(solution)/shard_map/factor/pallas_call | solution.py:104
  55.2 1.8 %collective-permute-done.33 = bf16[192,2048]{1,0:T(8,128)(2,1)S(1)} collective-permute-done((bf16[192,2048]{1,0:T(8,128)(2,1)S(1)}, bf16[192,2048]{1,0:T(8,128)(2,1)S(1)}, u32[]{:S(2)}, u32[]{:S(2)}) %collective-permute-start.33) | collective-permute-done | bytes 786464 | tf_op jit(solution)/shard_map/ppermute | solution.py:451
  57.2 9.0 %factor.5.refs_8_.refs_5_ = f32[192,1792]{1,0:T(8,128)S(1)} custom-call(bf16[48,4096]{1,0:T(8,128)(2,1)S(1)} %get-tuple-element.54.rest_0_.refs_0_, bf16[48,4096]{1,0:T(8,128)(2,1)S(1)} %collective-permute-done.27.rest_2_.refs_1_, bf16[48,4096]{1,0:T(8,128)(2,1)S(1)} %collective-permute-done.23.rest_1_.refs_2_, ...), custom_call_target="tpu_custom_call", output_to_operand_aliasing={{}: (7, {})} | custom-call | flops 3623878656 | bytes 18874368 | tf_op jit(solution)/shard_map/factor/pallas_call | solution.py:104
  68.9 5.0 %collective-permute-done.35.refs_3_ = bf16[48,4096]{1,0:T(8,128)(2,1)S(1)} collective-permute-done((bf16[48,4096]{1,0:T(8,128)(2,1)S(1)}, bf16[48,4096]{1,0:T(8,128)(2,1)S(1)}, u32[]{:S(2)}, u32[]{:S(2)}) %collective-permute-start.35) | collective-permute-done | bytes 393248 | tf_op jit(solution)/shard_map/ppermute | solution.py:418
  73.9 10.8 %factor.6.refs_10_.refs_7_.refs_4_ = f32[192,1792]{1,0:T(8,128)S(1)} custom-call(bf16[48,4096]{1,0:T(8,128)(2,1)S(1)} %collective-permute-done.24.refs_7_.refs_0_, bf16[48,4096]{1,0:T(8,128)(2,1)S(1)} %collective-permute-done.26.refs_5_.refs_9_.refs_1_, bf16[48,4096]{1,0:T(8,128)(2,1)S(1)} %collective-permute-done.25.refs_4_.refs_8_.refs_2_, ...), custom_call_target="tpu_custom_call" | custom-call | flops 4831838208 | bytes 25165824 | tf_op jit(solution)/shard_map/factor/pallas_call | solution.py:104
  89.2 10.6 %operand.3 = (bf16[192,1792]{1,0:T(8,128)(2,1)S(1)}, f32[16,128]{1,0:T(8,128)S(1)}) custom-call(bf16[48,4224]{1,0:T(8,128)(2,1)S(1)} %get-tuple-element.55.refs_10_.refs_0_, bf16[48,4224]{1,0:T(8,128)(2,1)S(1)} %collective-permute-done.28.refs_1_, bf16[48,4224]{1,0:T(8,128)(2,1)S(1)} %collective-permute-done.29.refs_7_.refs_2_, ...), custom_call_target="tpu_custom_call" | custom-call | flops 2818572288 | bytes 14680064 | tf_op jit(solution)/shard_map/operand/pallas_call | solution.py:154
  99.8 1.8 %collective-permute-start.44 = (bf16[192,1792]{1,0:T(8,128)(2,1)S(1)}, bf16[192,1792]{1,0:T(8,128)(2,1)}, u32[]{:S(2)}, u32[]{:S(2)}) collective-permute-start(bf16[192,1792]{1,0:T(8,128)(2,1)S(1)} %get-tuple-element.57.refs_8_.refs_6_.refs_1_), channel_id=1, source_target_pairs={{0,16},{8,24},{16,0},{24,8},{1,17},{9,25},{17,1},{25,9},{2,18},{10... | collective-permute-start | bytes 2064392 | tf_op jit(solution)/shard_map/ppermute | solution.py:463
  101.6 2.3 %collective-permute-start.38 = (bf16[48,4224]{1,0:T(8,128)(2,1)S(1)}, bf16[48,4224]{1,0:T(8,128)(2,1)S(1)}, u32[]{:S(2)}, u32[]{:S(2)}) collective-permute-start(bf16[48,4224]{1,0:T(8,128)(2,1)S(1)} %get-tuple-element.55.refs_10_.refs_0_), channel_id=1, source_target_pairs={{0,7},{1,6},{2,1},{3,0},{4,3},{5,2},{6,5},{7,4},{8,15},{9,14},{10,... | collective-permute-start | bytes 1216520 | tf_op jit(solution)/shard_map/ppermute | solution.py:416
  104.1 9.2 %factor.7.refs_5_.refs_1_ = f32[192,1792]{1,0:T(8,128)S(1)} custom-call(bf16[48,4096]{1,0:T(8,128)(2,1)S(1)} %collective-permute-done.24.refs_7_.refs_0_, bf16[48,4096]{1,0:T(8,128)(2,1)S(1)} %collective-permute-done.26.refs_5_.refs_9_.refs_1_, bf16[48,4096]{1,0:T(8,128)(2,1)S(1)} %collective-permute-done.25.refs_4_.refs_8_.refs_2_, ...), custom_call_target="tpu_custom_call", output_to_operand_aliasing={{}: (7, {})} | custom-call | flops 3623878656 | bytes 18874368 | tf_op jit(solution)/shard_map/factor/pallas_call | solution.py:104
  114.4 3.1 %collective-permute-done.44.refs_0_ = bf16[192,1792]{1,0:T(8,128)(2,1)} collective-permute-done((bf16[192,1792]{1,0:T(8,128)(2,1)S(1)}, bf16[192,1792]{1,0:T(8,128)(2,1)}, u32[]{:S(2)}, u32[]{:S(2)}) %collective-permute-start.44) | collective-permute-done | bytes 688160 | tf_op jit(solution)/shard_map/ppermute | solution.py:463
  118.3 2.0 %dynamic-slice_dynamic-update-slice_fusion = (bf16[384,1024]{1,0:T(8,128)(2,1)}, bf16[384,1024]{1,0:T(8,128)(2,1)}) fusion(bf16[384,1024]{1,0:T(8,128)(2,1)} %get-tuple-element.73, bf16[192,2048]{1,0:T(8,128)(2,1)} %collective-permute-done.39, s32[]{:T(128)S(6)} %select_n.80, bf16[384,1024]{1,0:T(8,128)(2,1)} %get-tuple-element.74, s32[]{:T(128)S(6)} %select_n.78), kind=kLoop, calls=%fused_computation.41 | loop fusion | bytes 1572872 | tf_op jit(solution)/shard_map/concatenate | solution.py:454
  122.2 7.1 %operand.4 = (bf16[192,1024]{1,0:T(8,128)(2,1)}, f32[16,128]{1,0:T(8,128)S(1)}) custom-call(bf16[48,4224]{1,0:T(8,128)(2,1)S(1)} %collective-permute-done.32.refs_6_.refs_0_, bf16[48,4224]{1,0:T(8,128)(2,1)S(1)} %collective-permute-done.36.refs_9_.refs_1_, bf16[48,4224]{1,0:T(8,128)(2,1)S(1)} %collective-permute-done.37.refs_10_.refs_2_, ...), custom_call_target="tpu_custom_call" | custom-call | flops 1610612736 | bytes 8388608 | tf_op jit(solution)/shard_map/operand/pallas_call | solution.py:154
  130.7 6.1 %operand.5.refs_5_.refs_1_ = bf16[192,768]{1,0:T(8,128)(2,1)} custom-call(bf16[48,4224]{1,0:T(8,128)(2,1)S(1)} %collective-permute-done.32.refs_6_.refs_0_, bf16[48,4224]{1,0:T(8,128)(2,1)S(1)} %collective-permute-done.36.refs_9_.refs_1_, bf16[48,4224]{1,0:T(8,128)(2,1)S(1)} %collective-permute-done.37.refs_10_.refs_2_, ...), custom_call_target="tpu_custom_call" | custom-call | flops 1207959552 | bytes 6291456 | tf_op jit(solution)/shard_map/operand/pallas_call | solution.py:154
  138.0 6.4 %hessian.3.refs_1_.refs_5_ = f32[1024,1792]{1,0:T(8,128)S(1)} custom-call(s32[1]{0:T(128)} %bitcast.6.dp_ref, bf16[1024,768]{1,0:T(8,128)(2,1)S(1)} %turn.3.refs_0_, bf16[192,1792]{1,0:T(8,128)(2,1)S(1)} %get-tuple-element.57.refs_8_.refs_6_.refs_1_, bf16[192,1792]{1,0:T(8,128)(2,1)} %after.2.refs_2_, bf16[192,1792]{1,0:T(8,128)(2,1)} %collective-permute-done.45.refs_3_, ...), custom_call_target="tpu_custom_call" | custom-call | flops 2818572288 | bytes 14680064 | tf_op jit(solution)/shard_map/hessian/pallas_call | solution.py:227
  144.4 3.0 %copy-done = f32[1024,1792]{1,0:T(8,128)} copy-done((f32[1024,1792]{1,0:T(8,128)}, f32[1024,1792]{1,0:T(8,128)S(1)}, u32[]{:S(2)}) %copy-start) | copy-done | bytes 7340056
  153.8 5.6 %hessian.4.refs_8_ = f32[1024,1792]{1,0:T(8,128)} custom-call(s32[1]{0:T(128)} %bitcast.6.dp_ref, bf16[1024,768]{1,0:T(8,128)(2,1)S(1)} %turn.2.refs_0_, bf16[192,1024]{1,0:T(8,128)(2,1)} %get-tuple-element.59.refs_6_.refs_1_, bf16[192,1024]{1,0:T(8,128)(2,1)S(1)} %copy-done.5, bf16[192,1024]{1,0:T(8,128)(2,1)} %collective-permute-done.48.refs_3_, ...), custom_call_target="tpu_custom_call" | custom-call | flops 1610612736 | bytes 8388608 | tf_op jit(solution)/shard_map/hessian/pallas_call | solution.py:227
  159.4 4.9 %hessian.5 = f32[1024,1792]{1,0:T(8,128)} custom-call(s32[1]{0:T(128)} %bitcast.6.dp_ref, bf16[1024,768]{1,0:T(8,128)(2,1)S(1)} %turn.2.refs_0_, bf16[192,768]{1,0:T(8,128)(2,1)} %operand.5.refs_5_.refs_1_, bf16[192,768]{1,0:T(8,128)(2,1)} %collective-permute-done.41.refs_8_.refs_2_, ...), custom_call_target="tpu_custom_call", output_to_operand_aliasing={{}: (9, {})} | custom-call | flops 1207959552 | bytes 6291456 | tf_op jit(solution)/shard_map/hessian/pallas_call | solution.py:227
  (121 shorter events, 35.9 us)
Async XLA Ops:
  4.9 15.0 %collective-permute-start.19 = (bf16[16,4096]{1,0:T(8,128)(2,1)S(1)}, bf16[16,4096]{1,0:T(8,128)(2,1)S(1)}, u32[]{:S(2)}, u32[]{:S(2)}) collective-permute-start(bf16[16,4096]{1,0:T(8,128)(2,1)S(1)} %get-tuple-element.50), channel_id=1, source_target_pairs={{0,24},{8,16},{16,8},{24,0},{1,25},{9,17},{17,9},{25,1},{2,26},{10... | collective-permute-start | bytes 393224 | tf_op jit(solution)/shard_map/ppermute | solution.py:475
  9.3 15.7 %collective-permute-start.23 = (bf16[48,4096]{1,0:T(8,128)(2,1)S(1)}, bf16[48,4096]{1,0:T(8,128)(2,1)S(1)}, u32[]{:S(2)}, u32[]{:S(2)}) collective-permute-start(bf16[48,4096]{1,0:T(8,128)(2,1)S(1)} %get-tuple-element.54.rest_0_.refs_0_), channel_id=1, source_target_pairs={{0,2},{1,3},{2,4},{3,5},{4,6},{5,7},{6,0},{7,1},{8,10},{9,11},{10,... | collective-permute-start | bytes 1179656 | tf_op jit(solution)/shard_map/ppermute | solution.py:413
  11.9 15.3 %collective-permute-start.27 = (bf16[48,4096]{1,0:T(8,128)(2,1)S(1)}, bf16[48,4096]{1,0:T(8,128)(2,1)S(1)}, u32[]{:S(2)}, u32[]{:S(2)}) collective-permute-start(bf16[48,4096]{1,0:T(8,128)(2,1)S(1)} %get-tuple-element.54.rest_0_.refs_0_), channel_id=1, source_target_pairs={{0,1},{1,0},{2,3},{3,2},{4,5},{5,4},{6,7},{7,6},{8,9},{9,8},{10,11... | collective-permute-start | bytes 1179656 | tf_op jit(solution)/shard_map/ppermute | solution.py:414
  25.0 14.2 %collective-permute-start.24 = (bf16[48,4096]{1,0:T(8,128)(2,1)S(1)}, bf16[48,4096]{1,0:T(8,128)(2,1)S(1)}, u32[]{:S(2)}, u32[]{:S(2)}) collective-permute-start(bf16[48,4096]{1,0:T(8,128)(2,1)S(1)} %collective-permute-done.23.rest_1_.refs_2_), channel_id=1, source_target_pairs={{0,2},{1,3},{2,4},{3,5},{4,6},{5,7},{6,0},{7,1},{8,10},{9,11},{10,... | collective-permute-start | bytes 1179656 | tf_op jit(solution)/shard_map/ppermute | solution.py:413
  37.8 19.2 %collective-permute-start.33 = (bf16[192,2048]{1,0:T(8,128)(2,1)S(1)}, bf16[192,2048]{1,0:T(8,128)(2,1)S(1)}, u32[]{:S(2)}, u32[]{:S(2)}) collective-permute-start(bf16[192,2048]{1,0:T(8,128)(2,1)S(1)} %columns.4), channel_id=1, source_target_pairs={{0,16},{8,24},{16,0},{24,8},{1,17},{9,25},{17,1},{25,9},{2,18},{10... | collective-permute-start | bytes 2359304 | tf_op jit(solution)/shard_map/ppermute | solution.py:451
  39.2 12.9 %collective-permute-start.25 = (bf16[48,4096]{1,0:T(8,128)(2,1)S(1)}, bf16[48,4096]{1,0:T(8,128)(2,1)S(1)}, u32[]{:S(2)}, u32[]{:S(2)}) collective-permute-start(bf16[48,4096]{1,0:T(8,128)(2,1)S(1)} %collective-permute-done.24.refs_7_.refs_0_), channel_id=1, source_target_pairs={{0,2},{1,3},{2,4},{3,5},{4,6},{5,7},{6,0},{7,1},{8,10},{9,11},{10,... | collective-permute-start | bytes 1179656 | tf_op jit(solution)/shard_map/ppermute | solution.py:413
  40.9 11.3 %collective-permute-start.26 = (bf16[48,4096]{1,0:T(8,128)(2,1)S(1)}, bf16[48,4096]{1,0:T(8,128)(2,1)S(1)}, u32[]{:S(2)}, u32[]{:S(2)}) collective-permute-start(bf16[48,4096]{1,0:T(8,128)(2,1)S(1)} %collective-permute-done.24.refs_7_.refs_0_), channel_id=1, source_target_pairs={{0,1},{1,0},{2,3},{3,2},{4,5},{5,4},{6,7},{7,6},{8,9},{9,8},{10,11... | collective-permute-start | bytes 1179656 | tf_op jit(solution)/shard_map/ppermute | solution.py:414
  53.1 13.1 %collective-permute-start.29 = (bf16[48,4224]{1,0:T(8,128)(2,1)S(1)}, bf16[48,4224]{1,0:T(8,128)(2,1)S(1)}, u32[]{:S(2)}, u32[]{:S(2)}) collective-permute-start(bf16[48,4224]{1,0:T(8,128)(2,1)S(1)} %get-tuple-element.55.refs_10_.refs_0_), channel_id=1, source_target_pairs={{0,2},{1,3},{2,4},{3,5},{4,6},{5,7},{6,0},{7,1},{8,10},{9,11},{10,... | collective-permute-start | bytes 1216520 | tf_op jit(solution)/shard_map/ppermute | solution.py:413
  53.2 34.8 %collective-permute-start.28 = (bf16[48,4224]{1,0:T(8,128)(2,1)S(1)}, bf16[48,4224]{1,0:T(8,128)(2,1)S(1)}, u32[]{:S(2)}, u32[]{:S(2)}) collective-permute-start(bf16[48,4224]{1,0:T(8,128)(2,1)S(1)} %get-tuple-element.55.refs_10_.refs_0_), channel_id=1, source_target_pairs={{0,1},{1,0},{2,3},{3,2},{4,5},{5,4},{6,7},{7,6},{8,9},{9,8},{10,11... | collective-permute-start | bytes 1216520 | tf_op jit(solution)/shard_map/ppermute | solution.py:414
  54.7 19.1 %collective-permute-start.35 = (bf16[48,4096]{1,0:T(8,128)(2,1)S(1)}, bf16[48,4096]{1,0:T(8,128)(2,1)S(1)}, u32[]{:S(2)}, u32[]{:S(2)}) collective-permute-start(bf16[48,4096]{1,0:T(8,128)(2,1)S(1)} %collective-permute-done.25.refs_4_.refs_8_.refs_2_), channel_id=1, source_target_pairs={{0,1},{1,0},{2,3},{3,2},{4,5},{5,4},{6,7},{7,6},{8,9},{9,8},{10,11... | collective-permute-start | bytes 1179656 | tf_op jit(solution)/shard_map/ppermute | solution.py:418
  57.1 32.1 %collective-permute-start.34 = (bf16[384,1024]{1,0:T(8,128)(2,1)S(1)}, bf16[384,1024]{1,0:T(8,128)(2,1)S(1)}, u32[]{:S(2)}, u32[]{:S(2)}) collective-permute-start(bf16[384,1024]{1,0:T(8,128)(2,1)S(1)} %get-tuple-element.71), channel_id=1, source_target_pairs={{0,8},{8,0},{16,24},{24,16},{1,9},{9,1},{17,25},{25,17},{2,10},{10... | collective-permute-start | bytes 2359304 | tf_op jit(solution)/shard_map/ppermute | solution.py:460
  66.2 23.0 %collective-permute-start.30 = (bf16[48,4224]{1,0:T(8,128)(2,1)S(1)}, bf16[48,4224]{1,0:T(8,128)(2,1)S(1)}, u32[]{:S(2)}, u32[]{:S(2)}) collective-permute-start(bf16[48,4224]{1,0:T(8,128)(2,1)S(1)} %collective-permute-done.29.refs_7_.refs_2_), channel_id=1, source_target_pairs={{0,1},{1,0},{2,3},{3,2},{4,5},{5,4},{6,7},{7,6},{8,9},{9,8},{10,11... | collective-permute-start | bytes 1216520 | tf_op jit(solution)/shard_map/ppermute | solution.py:414
  67.3 19.6 %collective-permute-start.32 = (bf16[48,4224]{1,0:T(8,128)(2,1)S(1)}, bf16[48,4224]{1,0:T(8,128)(2,1)S(1)}, u32[]{:S(2)}, u32[]{:S(2)}) collective-permute-start(bf16[48,4224]{1,0:T(8,128)(2,1)S(1)} %collective-permute-done.29.refs_7_.refs_2_), channel_id=1, source_target_pairs={{0,2},{1,3},{2,4},{3,5},{4,6},{5,7},{6,0},{7,1},{8,10},{9,11},{10,... | collective-permute-start | bytes 1216520 | tf_op jit(solution)/shard_map/ppermute | solution.py:413
  85.6 32.6 %collective-permute-start.39 = (bf16[192,2048]{1,0:T(8,128)(2,1)}, bf16[192,2048]{1,0:T(8,128)(2,1)}, u32[]{:S(2)}, u32[]{:S(2)}) collective-permute-start(bf16[192,2048]{1,0:T(8,128)(2,1)} %columns.5), channel_id=1, source_target_pairs={{0,16},{8,24},{16,0},{24,8},{1,17},{9,25},{17,1},{25,9},{2,18},{10... | collective-permute-start | bytes 2359304 | tf_op jit(solution)/shard_map/ppermute | solution.py:451
  86.9 17.1 %collective-permute-start.36 = (bf16[48,4224]{1,0:T(8,128)(2,1)S(1)}, bf16[48,4224]{1,0:T(8,128)(2,1)S(1)}, u32[]{:S(2)}, u32[]{:S(2)}) collective-permute-start(bf16[48,4224]{1,0:T(8,128)(2,1)S(1)} %collective-permute-done.32.refs_6_.refs_0_), channel_id=1, source_target_pairs={{0,1},{1,0},{2,3},{3,2},{4,5},{5,4},{6,7},{7,6},{8,9},{9,8},{10,11... | collective-permute-start | bytes 1216520 | tf_op jit(solution)/shard_map/ppermute | solution.py:414
  88.0 16.0 %collective-permute-start.37 = (bf16[48,4224]{1,0:T(8,128)(2,1)S(1)}, bf16[48,4224]{1,0:T(8,128)(2,1)S(1)}, u32[]{:S(2)}, u32[]{:S(2)}) collective-permute-start(bf16[48,4224]{1,0:T(8,128)(2,1)S(1)} %collective-permute-done.32.refs_6_.refs_0_), channel_id=1, source_target_pairs={{0,2},{1,3},{2,4},{3,5},{4,6},{5,7},{6,0},{7,1},{8,10},{9,11},{10,... | collective-permute-start | bytes 1216520 | tf_op jit(solution)/shard_map/ppermute | solution.py:413
  99.8 17.7 %collective-permute-start.44 = (bf16[192,1792]{1,0:T(8,128)(2,1)S(1)}, bf16[192,1792]{1,0:T(8,128)(2,1)}, u32[]{:S(2)}, u32[]{:S(2)}) collective-permute-start(bf16[192,1792]{1,0:T(8,128)(2,1)S(1)} %get-tuple-element.57.refs_8_.refs_6_.refs_1_), channel_id=1, source_target_pairs={{0,16},{8,24},{16,0},{24,8},{1,17},{9,25},{17,1},{25,9},{2,18},{10... | collective-permute-start | bytes 2064392 | tf_op jit(solution)/shard_map/ppermute | solution.py:463
  101.6 19.2 %collective-permute-start.38 = (bf16[48,4224]{1,0:T(8,128)(2,1)S(1)}, bf16[48,4224]{1,0:T(8,128)(2,1)S(1)}, u32[]{:S(2)}, u32[]{:S(2)}) collective-permute-start(bf16[48,4224]{1,0:T(8,128)(2,1)S(1)} %get-tuple-element.55.refs_10_.refs_0_), channel_id=1, source_target_pairs={{0,7},{1,6},{2,1},{3,0},{4,3},{5,2},{6,5},{7,4},{8,15},{9,14},{10,... | collective-permute-start | bytes 1216520 | tf_op jit(solution)/shard_map/ppermute | solution.py:416
  104.0 32.7 %collective-permute-start.45 = (bf16[192,1792]{1,0:T(8,128)(2,1)S(1)}, bf16[192,1792]{1,0:T(8,128)(2,1)}, u32[]{:S(2)}, u32[]{:S(2)}) collective-permute-start(bf16[192,1792]{1,0:T(8,128)(2,1)S(1)} %get-tuple-element.57.refs_8_.refs_6_.refs_1_), channel_id=1, source_target_pairs={{0,8},{8,0},{16,24},{24,16},{1,9},{9,1},{17,25},{25,17},{2,10},{10... | collective-permute-start | bytes 2064392 | tf_op jit(solution)/shard_map/ppermute | solution.py:467
  117.5 20.4 %collective-permute-start.46 = (bf16[192,1792]{1,0:T(8,128)(2,1)}, bf16[192,1792]{1,0:T(8,128)(2,1)S(1)}, u32[]{:S(2)}, u32[]{:S(2)}) collective-permute-start(bf16[192,1792]{1,0:T(8,128)(2,1)} %after.2.refs_2_), channel_id=1, source_target_pairs={{0,8},{8,0},{16,24},{24,16},{1,9},{9,1},{17,25},{25,17},{2,10},{10... | collective-permute-start | bytes 2064392 | tf_op jit(solution)/shard_map/ppermute | solution.py:467
  120.3 29.9 %collective-permute-start.40 = (bf16[384,1024]{1,0:T(8,128)(2,1)}, bf16[384,1024]{1,0:T(8,128)(2,1)}, u32[]{:S(2)}, u32[]{:S(2)}) collective-permute-start(bf16[384,1024]{1,0:T(8,128)(2,1)} %get-tuple-element.69), channel_id=1, source_target_pairs={{0,8},{8,0},{16,24},{24,16},{1,9},{9,1},{17,25},{25,17},{2,10},{10... | collective-permute-start | bytes 2359304 | tf_op jit(solution)/shard_map/ppermute | solution.py:460
  129.3 18.1 %collective-permute-start.47 = (bf16[192,1024]{1,0:T(8,128)(2,1)}, bf16[192,1024]{1,0:T(8,128)(2,1)S(1)}, u32[]{:S(2)}, u32[]{:S(2)}) collective-permute-start(bf16[192,1024]{1,0:T(8,128)(2,1)} %get-tuple-element.59.refs_6_.refs_1_), channel_id=1, source_target_pairs={{0,16},{8,24},{16,0},{24,8},{1,17},{9,25},{17,1},{25,9},{2,18},{10... | collective-permute-start | bytes 1179656 | tf_op jit(solution)/shard_map/ppermute | solution.py:463
  130.1 23.0 %collective-permute-start.48 = (bf16[192,1024]{1,0:T(8,128)(2,1)}, bf16[192,1024]{1,0:T(8,128)(2,1)}, u32[]{:S(2)}, u32[]{:S(2)}) collective-permute-start(bf16[192,1024]{1,0:T(8,128)(2,1)} %get-tuple-element.59.refs_6_.refs_1_), channel_id=1, source_target_pairs={{0,8},{8,0},{16,24},{24,16},{1,9},{9,1},{17,25},{25,17},{2,10},{10... | collective-permute-start | bytes 1179656 | tf_op jit(solution)/shard_map/ppermute | solution.py:467
  136.7 13.2 %collective-permute-start.41 = (bf16[192,768]{1,0:T(8,128)(2,1)}, bf16[192,768]{1,0:T(8,128)(2,1)}, u32[]{:S(2)}, u32[]{:S(2)}) collective-permute-start(bf16[192,768]{1,0:T(8,128)(2,1)} %operand.5.refs_5_.refs_1_), channel_id=1, source_target_pairs={{0,16},{8,24},{16,0},{24,8},{1,17},{9,25},{17,1},{25,9},{2,18},{10... | collective-permute-start | bytes 884744 | tf_op jit(solution)/shard_map/ppermute | solution.py:463
  (28 other events, 172.8 us)
